TPU v7x, 512 devices: a whole 4x4x16 slice. The times are simulated.
512 devices in a mesh: ctx: 64 (over x, z), ch: 8 (over y, core).
Axes of the slice: x: 4, y: 4, z: 16, core: 2. Of those that a mesh axis runs over, the one named last changes fastest.
Arguments:
- x_in: bfloat16 [8192, 8192], P('ctx', 'ch'), may hold values from -6 to 6
- gate_in: bfloat16 [8192, 8192], P('ctx', 'ch'), may hold values from -6 to 6
- conv_weight: float32 [4, 8192], P(None, 'ch'), may hold values from -3 to 3
- conv_bias: float32 [8192], P('ch'), may hold values from -3 to 3
- proj_low: bfloat16 [8192, 256], P('ch'), may hold values from -0.0625 to 0.0625
- proj_bc: bfloat16 [8192, 32], P('ch'), may hold values from -0.0625 to 0.0625
- dt_weight: bfloat16 [256, 8192], P(None, 'ch'), may hold values from -0.375 to 0.375
- dt_bias: float32 [8192], P('ch'), may hold values from -5 to -3
- decay_log: float32 [16, 8192], P(None, 'ch'), may hold values from -20 to 1.5
- skip_gain: float32 [8192], P('ch'), may hold values from 0.5 to 1.5
- attn_kv: bfloat16 [8192, 2048], P('ctx', 'ch'), may hold values from -6 to 6
- kept_index: int32 [8, 2048], P('ch', 'ctx'), may hold values from 0 to 8191, as said below
- kept_owner: int32 [8, 2048, 1], P('ch', 'ctx'), may hold values from 0 to 63; in each aligned block of 32 rows (0 to 31, 32 to 63, ..., all dimensions but the last counted through in order) at most 2 rows name the same one
Outputs:
- gated: bfloat16 [8192, 8192], P('ctx', 'ch')
- kept_cache: bfloat16 [8, 8192, 256], P('ch', 'ctx')
Inputs may be any that keep to these rules, and one draw needn't show every extreme that they name: `kept_index`: for head h, the block of entries i * 32 to (i + 1) * 32 - 1 holds distinct increasing positions in [i * 128, (i + 1) * 128) and always holds (i + 1) * 128 - 1. `kept_owner`: in each aligned block of 32 entries of a head no owner appears more than 2 times.
All inputs are finite; a program needn't handle non-finite values.
Results may differ from a plain program's by a relative error of at most 0.0062.
Values may be sent and summed in bfloat16 or wider, within the bound.
A program may use at most 64 MiB of HBM per device.

v0:
```python
import jax
import jax.numpy as jnp
from jax import lax
from jax.sharding import PartitionSpec as P

MOST = 2


def passed_along(value, axis, by):
    devices = lax.axis_size(axis)
    pairs = [(i, i + by) for i in range(devices) if 0 <= i + by < devices]
    return lax.ppermute(value, axis, pairs)


def prefix(value, axis, join, neutral):
    count, mine = (lax.axis_size(axis), lax.axis_index(axis))
    pieces = jax.tree.map(lambda part: lax.all_gather(part, axis), value)
    so_far = jax.tree.map(
        lambda part, zero: jnp.full_like(part, 0) + jnp.asarray(zero, part.dtype), value, neutral
    )

    def lap(position, so_far):
        longer = join(so_far, jax.tree.map(lambda part: part[position], pieces))
        return jax.tree.map(lambda new, old: jnp.where(position < mine, new, old), longer, so_far)

    return lax.fori_loop(0, count - 1, lap, so_far)


def scan_tokens(initial, step_size, b_coeff, c_coeff, x_float, decay_rate, turns):

    def advance(carry_state, inputs):
        step_row, b_row, c_row, x_row = inputs
        carry_state = (
            jnp.exp(-step_row[None, :] * decay_rate) * carry_state
            + (step_row * x_row)[None, :] * b_row[:, None]
        )
        return (carry_state, jnp.sum(c_row[:, None] * carry_state, axis=0))

    return lax.scan(advance, initial, (step_size, b_coeff, c_coeff, x_float), unroll=turns)


def final_state(initial, step_size, b_coeff, x_float, decay_rate, turns):

    def advance_only(carry_state, inputs):
        step_row, b_row, x_row = inputs
        carry_state = (
            jnp.exp(-step_row[None, :] * decay_rate) * carry_state
            + (step_row * x_row)[None, :] * b_row[:, None]
        )
        return (carry_state, None)

    result, _ = lax.scan(advance_only, initial, (step_size, b_coeff, x_float), unroll=turns)
    return result


def combine_states(earlier, later):
    return (earlier[0] * later[0], later[0] * earlier[1] + later[1])


def local(
    x_in,
    gate_in,
    conv_weight,
    conv_bias,
    proj_low,
    proj_bc,
    dt_weight,
    dt_bias,
    decay_log,
    skip_gain,
    attn_kv,
    kept_index,
    kept_owner,
):
    tok_rows, chan_width = x_in.shape
    conv_taps = conv_weight.shape[0]
    state_count = decay_log.shape[0]
    turns = max(16, tok_rows // 16)
    left_rim = passed_along(x_in[tok_rows - (conv_taps - 1) :], "ctx", 1)
    padded = jnp.concatenate([left_rim, x_in], axis=0)
    conv_sum = jnp.broadcast_to(conv_bias[None, :], (tok_rows, chan_width))
    for offset in range(conv_taps):
        conv_sum = conv_sum + conv_weight[offset][None, :] * padded[
            offset : offset + tok_rows
        ].astype(jnp.float32)
    conv_act = jax.nn.silu(conv_sum).astype(jnp.bfloat16)
    low_part = jnp.dot(conv_act, proj_low, preferred_element_type=jnp.float32)
    coeff_part = jnp.dot(conv_act, proj_bc, preferred_element_type=jnp.float32)
    low_total, coeff_total = lax.psum((low_part, coeff_part), "ch")
    low_rank = low_total.astype(jnp.bfloat16)
    state_in = coeff_total.astype(jnp.bfloat16)
    step_size = jax.nn.softplus(
        jnp.dot(low_rank, dt_weight, preferred_element_type=jnp.float32) + dt_bias[None, :]
    )
    decay_rate = jnp.exp(decay_log)
    b_coeff = state_in[:, :state_count].astype(jnp.float32)
    c_coeff = state_in[:, state_count:].astype(jnp.float32)
    x_float = conv_act.astype(jnp.float32)
    empty_state = jnp.zeros((state_count, chan_width), jnp.float32)
    local_end = final_state(empty_state, step_size, b_coeff, x_float, decay_rate, turns)
    decay_total = jnp.exp(-decay_rate * jnp.sum(step_size, axis=0)[None, :])
    _, carried = prefix(
        (decay_total, local_end),
        "ctx",
        combine_states,
        (jnp.ones_like(decay_total), jnp.zeros_like(local_end)),
    )
    _, outputs = scan_tokens(carried, step_size, b_coeff, c_coeff, x_float, decay_rate, turns)
    scanned = outputs + skip_gain[None, :] * x_float
    gated = (scanned * jax.nn.silu(gate_in.astype(jnp.float32))).astype(jnp.bfloat16)
    heads_dev, keep_count = kept_index.shape
    slot_total = lax.axis_size("ctx") * MOST
    row_base = lax.axis_index("ctx") * tok_rows
    local_pos = kept_index - row_base
    owner_ids = kept_owner[:, :, 0]
    same_owner = owner_ids[:, :, None] == owner_ids[:, None, :]
    earlier = jnp.arange(keep_count)[None, :] < jnp.arange(keep_count)[:, None]
    slot_rank = jnp.sum(jnp.where(same_owner & earlier[None], 1, 0), axis=2).astype(jnp.int32)
    slot_index = owner_ids * MOST + slot_rank
    dest_onehot = (
        slot_index[:, :, None] == jnp.arange(slot_total, dtype=jnp.int32)[None, None, :]
    ).astype(jnp.bfloat16)
    source_onehot = (
        local_pos[:, :, None] == jnp.arange(tok_rows, dtype=jnp.int32)[None, None, :]
    ).astype(jnp.bfloat16)
    selector = jnp.einsum(
        "hks,hkt->hst", dest_onehot, source_onehot, preferred_element_type=jnp.float32
    ).astype(jnp.bfloat16)
    kv_heads = attn_kv.reshape(tok_rows, heads_dev, -1)
    outgoing = jnp.einsum(
        "hst,thc->hsc", selector, kv_heads, preferred_element_type=jnp.float32
    ).astype(jnp.bfloat16)
    kept_cache = lax.all_to_all(outgoing, "ctx", split_axis=1, concat_axis=1, tiled=True)
    return (gated, kept_cache)


def solution(mesh):
    return jax.shard_map(
        local,
        mesh=mesh,
        in_specs=(
            P("ctx", "ch"),
            P("ctx", "ch"),
            P(None, "ch"),
            P("ch"),
            P("ch", None),
            P("ch", None),
            P(None, "ch"),
            P("ch"),
            P(None, "ch"),
            P("ch"),
            P("ctx", "ch"),
            P("ch", "ctx"),
            P("ch", "ctx", None),
        ),
        out_specs=(P("ctx", "ch"), P("ch", "ctx", None)),
        check_vma=False,
    )
```

profile of v0, /device:TPU:8, one launch (start us, length us, event | category | flops | bytes accessed | tf_op | source)
XLA Modules:
  0.0 426.0 jit_solution(16501119273952408715)
XLA Ops:
  8.0 3.8 collective-permute-start
  13.2 1.7 multiply_convert_fusion
  14.9 1.3 fusion.161
  16.2 1.0 fusion.162
  17.2 24.8 %all-reduce.2 = (bf16[128,256]{1,0:T(8,128)(2,1)S(1)}, bf16[128,32]{0,1:T(8,128)(2,1)S(1)}) all-reduce(f32[128,256]{1,0:T(8,128)S(1)} %fusion.161, f32[128,32]{0,1:T(8,128)S(1)} %fusion.162), channel_id=1, replica_groups=mesh['ctx'=64,'ch'=8] {'ch'}, use_global_device_ids=true, to_apply=%region_0.1 | all-reduce | flops 36864 | bytes 221184 | tf_op jit(solution)/shard_map/psum | solution.py:89
  42.3 1.2 fusion.160
  44.1 5.6 %while.38 = (s32[]{:T(128)}, f32[16,1024]{1,0:T(8,128)S(1)}, f32[8,16,1024]{2,1,0:T(8,128)S(1)}, f32[16,1024]{1,0:T(8,128)S(1)}, f32[8,16,1024]{2,1,0:T(8,128)S(...) while((s32[]{:T(128)}, f32[16,1024]{1,0:T(8,128)S(1)}, ...), condition=%wide.region_4.5_spmd.clone, body=%wide.region_3.4_spmd.clone.sunk | while | flops 1097746 | bytes 593419 | solution.py:52
  52.4 1.0 reduce.1
  54.1 18.6 %all-to-all-start = ((bf16[64,2,256]{2,1,0:T(2,128)(2,1)}), bf16[64,2,256]{2,1,0:T(2,128)(2,1)S(1)}, u32[]{:S(2)}, u32[]{:S(2)}) async-start(bf16[64,2,256]{2,1,0:T(2,128)(2,1)} %reshape.1108), calls=%async_computation | async-start | bytes 131072 | tf_op jit(solution)/shard_map/all_to_all | solution.py:133
  72.8 14.6 %all-to-all-done = bf16[64,2,256]{2,1,0:T(2,128)(2,1)S(1)} async-done(((bf16[64,2,256]{2,1,0:T(2,128)(2,1)}), bf16[64,2,256]{2,1,0:T(2,128)(2,1)S(1)}, u32[]{:S(2)}, u32[]{:S(2)}) %all-to-all-start) | async-done | bytes 65568 | tf_op jit(solution)/shard_map/all_to_all | solution.py:133
  88.0 114.4 %all-gather.7.cloned.1.call-done = f32[1024,1024]{1,0:T(8,128)} async-done(((f32[16,1024]{1,0:T(8,128)}), f32[1024,1024]{1,0:T(8,128)}) %all-gather.7.cloned.1.call-update) | async-done | bytes 4194320 | tf_op jit(solution)/shard_map/all_gather | solution.py:17
  202.4 144.7 %all-gather.5.cloned.1.call-done = f32[1024,1024]{1,0:T(8,128)} async-done(((f32[16,1024]{1,0:T(8,128)}), f32[1024,1024]{1,0:T(8,128)}) %all-gather.5.cloned.1.call-update) | async-done | bytes 4194320 | tf_op jit(solution)/shard_map/all_gather | solution.py:17
  347.2 59.0 %while.39 = (s32[]{:T(128)}, f32[16,1024]{1,0:T(8,128)S(1)}, s32[]{:T(128)}, f32[64,16,1024]{2,1,0:T(8,128)}, f32[64,16,1024]{2,1,0:T(8,128)}, /*index=5*/s32[]{:T(128)}, s32[]{:T(128)}) while((s32[]{:T(128)}, f32[16,1024]{1,0:T(8,128)S(1)}, s32[]{:T(128)}, f32[64,16,1024]{2,1,0:T(8,128)}, f32[64,16,1024]{2,1,0:T(8,128)}, ...), condition=%wide.region_6.7_spmd.clone, body=%wide.region_5.6_spmd.clone.sunk | while | flops 65540 | bytes 262245 | solution.py:26
  348.1 0.9 fusion.179
  349.0 0.9 fusion.179
  350.0 0.9 fusion.179
  350.9 0.9 fusion.179
  351.9 0.9 fusion.179
  352.8 0.9 fusion.179
  353.7 0.9 fusion.179
  354.7 0.9 fusion.179
  355.6 0.9 fusion.179
  356.5 0.9 fusion.179
  357.5 0.9 fusion.179
  358.4 0.9 fusion.179
  359.4 0.9 fusion.179
  360.3 0.9 fusion.179
  361.2 0.9 fusion.179
  362.2 0.9 fusion.179
  363.1 0.9 fusion.179
  364.0 0.9 fusion.179
  365.0 0.9 fusion.179
  365.9 0.9 fusion.179
  366.9 0.9 fusion.179
  367.8 0.9 fusion.179
  368.7 0.9 fusion.179
  369.7 0.9 fusion.179
  370.6 0.9 fusion.179
  371.5 0.9 fusion.179
  372.5 0.9 fusion.179
  373.4 0.9 fusion.179
  374.4 0.9 fusion.179
  375.3 0.9 fusion.179
  376.2 0.9 fusion.179
  377.2 0.9 fusion.179
  378.1 0.9 fusion.179
  379.0 0.9 fusion.179
  380.0 0.9 fusion.179
  380.9 0.9 fusion.179
  381.9 0.9 fusion.179
  382.8 0.9 fusion.179
  383.7 0.9 fusion.179
  384.7 0.9 fusion.179
  385.6 0.9 fusion.179
  386.5 0.9 fusion.179
  387.5 0.9 fusion.179
  388.4 0.9 fusion.179
  389.4 0.9 fusion.179
  390.3 0.9 fusion.179
  391.2 0.9 fusion.179
  393.1 0.9 fusion.179
  397.8 0.9 fusion.179
  404.4 0.9 fusion.179
  406.2 12.0 %while.37 = (s32[]{:T(128)}, f32[16,1024]{1,0:T(8,128)S(1)}, f32[8,16,1024]{2,1,0:T(8,128)S(1)}, f32[8,16,1024]{2,1,0:T(8,128)S(1)}, f32[16,1024]{1,0:T(8,128)S(...) while((s32[]{:T(128)}, f32[16,1024]{1,0:T(8,128)S(1)}, ...), condition=%wide.region_24.25_spmd, body=%wide.region_7.24_spmd.sunk | while | flops 2375697 | bytes 1744149 | solution.py:39
  (150 shorter events, 36.7 us)
Async XLA Ops:
  7.2 35.1 %copy-start = (bf16[256,1024]{1,0:T(8,128)(2,1)S(1)}, bf16[256,1024]{1,0:T(8,128)(2,1)}, u32[]{:S(2)}) copy-start(bf16[256,1024]{1,0:T(8,128)(2,1)} %param.25) | copy-start | bytes 1572868
  7.2 36.3 %copy-start.2 = (f32[16,1024]{1,0:T(8,128)S(1)}, f32[16,1024]{1,0:T(8,128)}, u32[]{:S(2)}) copy-start(f32[16,1024]{1,0:T(8,128)} %param.27) | copy-start | bytes 196612
  7.2 195.3 %all-gather.7.cloned.1.call-start = ((), (), s32[]{:S(2)}) async-start(), calls=%async_computation.2 | async-start | bytes 4259840 | tf_op jit(solution)/shard_map/all_gather | solution.py:17
  8.0 5.2 %collective-permute-start = (bf16[3,1024]{1,0:T(4,128)(2,1)S(1)}, bf16[3,1024]{1,0:T(4,128)(2,1)S(1)}, u32[]{:S(2)}, u32[]{:S(2)}) collective-permute-start(bf16[3,1024]{1,0:T(4,128)(2,1)S(1)} %slice.479), channel_id=1, source_target_pairs={{0,8},{8,16},{16,24},{24,32},{32,40},{40,48},{48,56},{56,64},{64,7... | collective-permute-start | bytes 18440 | tf_op jit(solution)/shard_map/ppermute | solution.py:12
  42.2 9.0 %copy-start.7 = (s32[1,32,1]{1,2,0:T(1,128)S(1)}, s32[1,32,1]{1,2,0:T(1,128)}, u32[]{:S(2)}) copy-start(s32[1,32,1]{1,2,0:T(1,128)} %param.31) | copy-start | bytes 388
  42.2 9.1 %copy-start.6 = (s32[1,32]{1,0:T(1,128)S(1)}, s32[1,32]{1,0:T(1,128)}, u32[]{:S(2)}) copy-start(s32[1,32]{1,0:T(1,128)} %param.30) | copy-start | bytes 388
  42.2 9.2 %copy-start.3 = (bf16[128,256]{1,0:T(8,128)(2,1)S(1)}, bf16[128,256]{1,0:T(8,128)(2,1)}, u32[]{:S(2)}) copy-start(bf16[128,256]{1,0:T(8,128)(2,1)} %param.29) | copy-start | bytes 196612
  49.7 0.6 copy-start.4
  50.4 296.8 %all-gather.5.cloned.1.call-start = ((), (), s32[]{:S(2)}) async-start(), calls=%async_computation.1 | async-start | bytes 4259840 | tf_op jit(solution)/shard_map/all_gather | solution.py:17
  54.1 33.3 %all-to-all-start = ((bf16[64,2,256]{2,1,0:T(2,128)(2,1)}), bf16[64,2,256]{2,1,0:T(2,128)(2,1)S(1)}, u32[]{:S(2)}, u32[]{:S(2)}) async-start(bf16[64,2,256]{2,1,0:T(2,128)(2,1)} %reshape.1108), calls=%async_computation | async-start | bytes 131072 | tf_op jit(solution)/shard_map/all_to_all | solution.py:133
  406.2 12.0 %copy-start.1 = (bf16[128,1024]{1,0:T(8,128)(2,1)S(1)}, bf16[128,1024]{1,0:T(8,128)(2,1)}, u32[]{:S(2)}) copy-start(bf16[128,1024]{1,0:T(8,128)(2,1)} %param.20) | copy-start | bytes 786436
  406.2 12.0 %copy-start.5 = (f32[1024]{0:T(1024)S(1)}, f32[1024]{0:T(1024)}, u32[]{:S(2)}) copy-start(f32[1024]{0:T(1024)} %param.28) | copy-start | bytes 12292
Sparse Core Ops, SparseCore 0:
  50.5 151.8 all-gather.6
  206.0 141.1 all-gather.4
where the time goes:
time: 429 us; the launch traced here: 426 us
  waiting for transfers between devices  275 us (64%)
  other arithmetic  75.9 us (18%)
  blocking collectives  24.8 us (6%)
  starting transfers between devices  22.5 us (5%)
  between operations  14.3 us (3%)
  local copies, waits for them, and re-layouts  7.67 us (2%)
    all_gather x2, waiting for transfers between devices, prefix(): pieces = jax.tree.map(lambda part: lax.all_gather(part, axis), value)  259 us
    select_n x63, other arithmetic, lap(): jnp.where(position < mine, new, old)  57.7 us
    psum x1, blocking collectives, local(): low_total, coeff_total = lax.psum((low_part, coeff_part), 'ch')  24.8 us
    all_to_all x1, starting transfers between devices, local(): lax.all_to_all(outgoing, 'ctx', split_axis=1, concat_axis=1, tiled=True)  18.6 us
    all_to_all x1, waiting for transfers between devices, local(): lax.all_to_all(outgoing, 'ctx', split_axis=1, concat_axis=1, tiled=True)  14.6 us
  transfers between devices with their start and end apart: 4, of which 4 were waited for; matrix products, arithmetic and copies ran while one was open for 1% of the time, Pallas kernels for 0%

commit v1 on v0

v1 whole, which is shorter than its diff:
```python
import functools
import math

import jax
import jax.numpy as jnp
from jax import lax
from jax.experimental import pallas as pl
from jax.experimental.pallas import tpu as pltpu
from jax.sharding import PartitionSpec as P

MOST = 2
NZ = 16
NX = 4
NC = 8
TOK = 128
CH = 1024
ST = 16
CONV = 4
RANK = 256
LANES = 128
TILES = CH // LANES
KEEP = 32
F32 = jnp.float32
BF16 = jnp.bfloat16
LOG2E = math.log2(math.e)


def dot(a, b):
    return jnp.dot(a, b, preferred_element_type=F32)


def dot_rows(a, b):
    return lax.dot_general(a, b, (((0,), (0,)), ((), ())), preferred_element_type=F32)


def silu(v):
    return v / (1.0 + jnp.exp(-v))


def iota(shape, dim):
    return lax.broadcasted_iota(jnp.int32, shape, dim)


def kernel(
    x_hbm, gate_hbm, cw_hbm, cb_hbm, low_hbm, bc_hbm, dtw_hbm, dtb_hbm, dec_hbm, skip_hbm, kv_hbm, idx_hbm, own_hbm,
    gated_out, kept_out,
    x_v, gate_v, cw_v, cb_v, low_v, bc_v, dtw_v, dtb_v, dec_v, skip_v, kv_v, idx_v, own_v, decs_v,
    halo, xs, act, part, rs_in, ag_out, lr, dtb3, xb3, bcx, a2b, lb, gb, yb, sg,
    s_out, s_in, l_out, l_in, sx_out, sx_in, t_out, t_in, h_out, h_in,
    kz_out, kz_in, kx_out,
    in_sem, send_sem, recv_sem,
):
    kx_in = kept_out.at[0]
    me = lax.axis_index("ctx")
    mc = lax.axis_index("ch")
    mx = me // NZ
    mz = me % NZ
    mj = mz // 2
    mhalf = mz % 2

    loads = [
        (x_hbm, x_v), (cw_hbm, cw_v), (cb_hbm, cb_v), (idx_hbm, idx_v), (own_hbm, own_v), (kv_hbm, kv_v),
        (low_hbm, low_v), (bc_hbm, bc_v), (dec_hbm, dec_v),
        (dec_hbm.at[pl.ds(mhalf * 8, 8), pl.ds(pl.multiple_of(mj * LANES, LANES), LANES)], decs_v),
        (dtw_hbm, dtw_v), (dtb_hbm, dtb_v), (skip_hbm, skip_v), (gate_hbm, gate_v),
    ]
    loads = [pltpu.make_async_copy(s, d, in_sem.at[i]) for i, (s, d) in enumerate(loads)]
    (x_ld, cw_ld, cb_ld, idx_ld, own_ld, kv_ld, low_ld, bc_ld, dec_ld, decs_ld, dtw_ld, dtb_ld, skip_ld, gate_ld) = loads

    for c in loads:
        c.start()

    barrier = pltpu.get_barrier_semaphore()
    for d in range(1, NZ):
        pl.semaphore_signal(barrier, inc=1, device_id={"ctx": mx * NZ + (mz + d) % NZ})
    for d in range(1, NX):
        pl.semaphore_signal(barrier, inc=1, device_id={"ctx": ((mx + d) % NX) * NZ + mz})
    for d in range(1, NC):
        pl.semaphore_signal(barrier, inc=1, device_id={"ch": (mc + d) % NC})
    right = (me + 1) % (NX * NZ)
    left = (me + NX * NZ - 1) % (NX * NZ)

    @pl.when(mz == NZ - 1)
    def _():
        pl.semaphore_signal(barrier, inc=1, device_id={"ctx": right})

    @pl.when(mz == 0)
    def _():
        pl.semaphore_signal(barrier, inc=1, device_id={"ctx": left})

    pl.semaphore_wait(barrier, NZ - 1 + NX - 1 + NC - 1 + jnp.where((mz == 0) | (mz == NZ - 1), 1, 0))

    def remote(src, dst, k, peer):
        return pltpu.make_async_remote_copy(
            src_ref=src, dst_ref=dst, send_sem=send_sem.at[k], recv_sem=recv_sem.at[k], device_id=peer
        )

    def drain(ref, sem):
        pltpu.make_async_copy(ref, ref, sem).wait()

    HALO, RS, AG, KZ, KX, SZ, LZ, SX, TX, HZ = range(10)

    remote(x_hbm.at[pl.ds(TOK - 16, 16), :], halo, HALO, {"ctx": right}).start()

    x_ld.wait()
    cw_ld.wait()
    cb_ld.wait()
    xs[pl.ds(16, TOK), :] = x_v[...].astype(F32)
    for j in range(TILES):
        cols = pl.ds(j * LANES, LANES)
        s = jnp.broadcast_to(cb_v[:, cols], (TOK - 16, LANES))
        for k in range(CONV):
            s = s + cw_v[pl.ds(k, 1), cols] * xs[pl.ds(32 - (CONV - 1) + k, TOK - 16), cols]
        a = silu(s).astype(BF16)
        act[pl.ds(16, TOK - 16), cols] = a
        xb3[pl.ds(16 * TILES + j, TOK - 16, stride=TILES), :] = a.astype(F32)

    idx_ld.wait()
    own_ld.wait()
    kv_ld.wait()
    own_row = own_v[...]
    eye = iota((KEEP, KEEP), 0) == iota((KEEP, KEEP), 1)
    own = jnp.sum(jnp.where(eye, own_row, 0), axis=1, keepdims=True)
    same = (own_row == own) & (iota((KEEP, KEEP), 1) < iota((KEEP, KEEP), 0))
    rank = jnp.sum(jnp.where(same, 1, 0), axis=1, keepdims=True)
    place = (own & (NZ - 1)) * 16 + (own >> 4) * 2 + rank
    src_t = (iota((TOK, KEEP), 0) == idx_v[...] - me * TOK).astype(F32).astype(BF16)
    picked = dot_rows(src_t, kv_v[...]).astype(BF16)
    slots = iota((KEEP, 256), 1)
    kz = dot_rows((slots == place).astype(F32).astype(BF16), picked[:, :LANES])
    kz = kz + dot_rows((slots == place + 8).astype(F32).astype(BF16), picked[:, LANES:])
    kz_out[...] = kz.astype(BF16)

    drain(halo, recv_sem.at[HALO])
    xs[pl.ds(0, 16), :] = jnp.where(me > 0, halo[...].astype(F32), 0.0)
    for j in range(TILES):
        cols = pl.ds(j * LANES, LANES)
        s = jnp.broadcast_to(cb_v[:, cols], (16, LANES))
        for k in range(CONV):
            s = s + cw_v[pl.ds(k, 1), cols] * xs[pl.ds(16 - (CONV - 1) + k, 16), cols]
        a = silu(s).astype(BF16)
        act[pl.ds(0, 16), cols] = a
        xb3[pl.ds(j, 16, stride=TILES), :] = a.astype(F32)

    low_ld.wait()
    bc_ld.wait()
    part[:, pl.ds(RANK, LANES)] = jnp.zeros((TOK, LANES), F32)
    part[:, pl.ds(0, RANK)] = dot(act[...], low_v[...])
    part[:, pl.ds(RANK, 2 * ST)] = lax.dot_general(
        act[...], bc_v[...], (((1,), (1,)), ((), ())), preferred_element_type=F32
    )

    def rows_of(i):
        return pl.ds(pl.multiple_of(i * 16, 16), 16)

    for d in range(1, NC):
        to = (mc + d) % NC
        remote(part.at[rows_of(to), :], rs_in.at[rows_of(mc), :], RS, {"ch": to}).start()
    rs_in[rows_of(mc), :] = part[rows_of(mc), :]
    for d in range(1, NZ):
        to = (mz + d) % NZ
        remote(kz_out.at[rows_of(to), :], kz_in.at[rows_of(mz), :], KZ, {"ctx": mx * NZ + to}).start()
    kz_in[rows_of(mz), :] = kz_out[rows_of(mz), :]

    dec_ld.wait()
    decs_ld.wait()
    gate_ld.wait()
    for j in range(TILES):
        a2b[pl.ds(j, ST, stride=TILES), :] = -LOG2E * jnp.exp(dec_v[:, pl.ds(j * LANES, LANES)])
    a2s = -LOG2E * jnp.exp(decs_v[...])
    sg[...] = silu(gate_v[...].astype(F32))

    drain(rs_in.at[pl.ds(0, TOK - 16), :], recv_sem.at[RS])
    total = rs_in[pl.ds(0, 16), :]
    for i in range(1, NC):
        total = total + rs_in[pl.ds(16 * i, 16), :]
    ag_out[...] = total.astype(BF16)
    for d in range(1, NC):
        to = (mc + d) % NC
        remote(ag_out, lr.at[rows_of(mc), :], AG, {"ch": to}).start()
    lr[rows_of(mc), :] = ag_out[...]

    drain(kz_in.at[pl.ds(0, 240), :], recv_sem.at[KZ])
    row = iota((TOK, 256), 0)
    want = ((row >> 1) & (NZ - 1)) * 16 + (row >> 5) * 2 + (row & 1)
    for half in range(2):
        sel = (iota((TOK, 256), 1) == want + half * 8).astype(F32).astype(BF16)
        kx_out[:, pl.ds(half * LANES, LANES)] = dot(sel, kz_in[...]).astype(BF16)

    def block_of(i):
        return pl.ds(pl.multiple_of(i * 32, 32), 32)

    for d in range(1, NX):
        to = (mx + d) % NX
        remote(kx_out.at[block_of(to), :], kx_in.at[block_of(mx), :], KX, {"ctx": to * NZ + mz}).start()
    kx_in[block_of(mx), :] = kx_out[block_of(mx), :]

    dtw_ld.wait()
    dtb_ld.wait()
    skip_ld.wait()
    drain(lr.at[pl.ds(0, TOK - 16), :], recv_sem.at[AG])

    for j in range(TILES):
        cols = pl.ds(j * LANES, LANES)
        v = dot(lr[:, pl.ds(0, RANK)], dtw_v[:, cols]) + dtb_v[:, cols]
        dtb3[pl.ds(j, TOK, stride=TILES), :] = jnp.maximum(v, 0.0) + jnp.log1p(jnp.exp(-jnp.abs(v)))
    coeff = lr[:, pl.ds(RANK, LANES)][:, : 2 * ST]
    for i in range(8):
        spread = (iota((2 * ST, 4 * LANES), 1) >> 7) + 4 * i == iota((2 * ST, 4 * LANES), 0)
        bcx[:, :, pl.ds(i * 4 * LANES, 4 * LANES)] = dot(coeff, spread.astype(F32).astype(BF16)).reshape(TOK // 8, 8, 4 * LANES)

    def total_step(t, acc):
        for u in range(8):
            acc = acc + dtb3[pl.ds(pl.multiple_of(t * 64, 64) + u * 8, 8), :]
        return acc

    s_total = lax.fori_loop(0, TOK // 8, total_step, jnp.zeros((TILES, LANES), F32))
    for j in range(TILES):
        s_out[j] = s_total[j : j + 1, :]
    for d in range(1, NZ):
        to = (mz + d) % NZ
        remote(s_out.at[to // 2], s_in.at[mz], SZ, {"ctx": mx * NZ + to}).start()
    s_in[mz] = s_out[mj]

    def scan_step(g, state):
        state = list(state)
        for u in range(8):
            dt = dtb3[pl.ds(pl.multiple_of(g * 64, 64) + u * 8, 8), :]
            xt = xb3[pl.ds(pl.multiple_of(g * 64, 64) + u * 8, 8), :]
            dx = dt * xt
            y = [None] * 4
            for n in range(ST):
                b = bcx[g, pl.ds(u, 1), pl.ds(n * LANES, LANES)]
                c = bcx[g, pl.ds(u, 1), pl.ds((ST + n) * LANES, LANES)]
                state[n] = jnp.exp2(dt * a2b[pl.ds(n * 8, 8), :]) * state[n] + dx * b
                term = c * state[n]
                y[n % 4] = term if y[n % 4] is None else y[n % 4] + term
            yb[pl.ds(pl.multiple_of(g * 64, 64) + u * 8, 8), :] = (y[0] + y[1]) + (y[2] + y[3])
        return tuple(state)

    state = lax.fori_loop(0, TOK // 8, scan_step, tuple(jnp.zeros((TILES, LANES), F32) for _ in range(ST)))
    for n in range(ST):
        lb[pl.ds(n * 8, 8), :] = state[n]
    for j in range(TILES):
        l_out[pl.ds(j * ST, ST), :] = lb[pl.ds(j, ST, stride=TILES), :]

    def tile_of(i):
        return pl.ds(pl.multiple_of(i * 8, 8), 8)

    for d in range(1, NZ):
        to = (mz + d) % NZ
        remote(l_out.at[tile_of(to), :], l_in.at[tile_of(mz), :], LZ, {"ctx": mx * NZ + to}).start()
    l_in[tile_of(mz), :] = l_out[tile_of(mz), :]

    drain(s_in.at[pl.ds(0, NZ - 1)], recv_sem.at[SZ])
    run = jnp.zeros((1, LANES), F32)
    decay, reach = [], []
    for z in range(NZ):
        decay.append(jnp.exp2(a2s * s_in[z]))
        reach.append(jnp.exp2(a2s * run))
        run = run + s_in[z]
    sx_out[...] = run
    for d in range(1, NX):
        remote(sx_out, sx_in.at[mx], SX, {"ctx": ((mx + d) % NX) * NZ + mz}).start()
    sx_in[mx] = run

    def reach_step(g, cum):
        for u in range(8):
            cum = cum + dtb3[pl.ds(pl.multiple_of(g * 64, 64) + u * 8, 8), :]
            for n in range(ST):
                c = bcx[g, pl.ds(u, 1), pl.ds((ST + n) * LANES, LANES)]
                gb[pl.ds(pl.multiple_of(g * 1024, 1024) + u * 128 + n * 8, 8), :] = c * jnp.exp2(cum * a2b[pl.ds(n * 8, 8), :])
        return cum

    drain(l_in.at[pl.ds(0, TOK - 8), :], recv_sem.at[LZ])
    before = []
    carry = jnp.zeros((8, LANES), F32)
    for z in range(NZ):
        before.append(carry)
        carry = decay[z] * carry + l_in[pl.ds(z * 8, 8), :]
    t_out[...] = carry
    for d in range(1, NX):
        remote(t_out, t_in.at[mx], TX, {"ctx": ((mx + d) % NX) * NZ + mz}).start()
    t_in[mx] = carry

    lax.fori_loop(0, TOK // 8, reach_step, jnp.zeros((TILES, LANES), F32))

    drain(sx_in.at[pl.ds(0, NX - 1)], recv_sem.at[SX])
    drain(t_in.at[pl.ds(0, NX - 1)], recv_sem.at[TX])
    plane = jnp.zeros((8, LANES), F32)
    for i in range(NX - 1):
        plane = jnp.where(i < mx, jnp.exp2(a2s * sx_in[i]) * plane + t_in[i], plane)
    for z in range(NZ):
        h_out[pl.ds(z * 8, 8), :] = before[z] + reach[z] * plane
    for d in range(1, NZ):
        to = (mz + d) % NZ
        remote(h_out.at[tile_of(to), :], h_in.at[tile_of(mz), :], HZ, {"ctx": mx * NZ + to}).start()
    h_in[tile_of(mz), :] = h_out[tile_of(mz), :]
    drain(h_in.at[pl.ds(0, TOK - 8), :], recv_sem.at[HZ])

    carried = [h_in[pl.ds(n, TILES, stride=ST), :] for n in range(ST)]

    def add_step(g, _):
        for u in range(8):
            at = pl.ds(pl.multiple_of(g * 64, 64) + u * 8, 8)
            y = [yb[at, :], None, None, None]
            for n in range(ST):
                term = gb[pl.ds(pl.multiple_of(g * 1024, 1024) + u * 128 + n * 8, 8), :] * carried[n]
                y[n % 4] = term if y[n % 4] is None else y[n % 4] + term
            yb[at, :] = (y[0] + y[1]) + (y[2] + y[3])
        return 0

    lax.fori_loop(0, TOK // 8, add_step, 0)

    for j in range(TILES):
        cols = pl.ds(j * LANES, LANES)
        y = yb[pl.ds(j, TOK, stride=TILES), :] + skip_v[:, cols] * act[:, cols].astype(F32)
        gated_out[:, cols] = (y * sg[:, cols]).astype(BF16)
    drain(kx_in.at[pl.ds(0, 96), :], recv_sem.at[KX])

    drain(halo, send_sem.at[HALO])
    drain(rs_in.at[pl.ds(0, TOK - 16), :], send_sem.at[RS])
    drain(lr.at[pl.ds(0, TOK - 16), :], send_sem.at[AG])
    drain(kz_in.at[pl.ds(0, 240), :], send_sem.at[KZ])
    drain(kx_in.at[pl.ds(0, 96), :], send_sem.at[KX])
    drain(s_in.at[pl.ds(0, NZ - 1)], send_sem.at[SZ])
    drain(l_in.at[pl.ds(0, TOK - 8), :], send_sem.at[LZ])
    drain(sx_in.at[pl.ds(0, NX - 1)], send_sem.at[SX])
    drain(t_in.at[pl.ds(0, NX - 1)], send_sem.at[TX])
    drain(h_in.at[pl.ds(0, TOK - 8), :], send_sem.at[HZ])


def local(
    x_in, gate_in, conv_weight, conv_bias, proj_low, proj_bc, dt_weight, dt_bias, decay_log, skip_gain, attn_kv,
    kept_index, kept_owner,
):
    V = pltpu.VMEM
    hbm = pl.BlockSpec(memory_space=pltpu.HBM)
    return pl.pallas_call(
        kernel,
        out_shape=(jax.ShapeDtypeStruct((TOK, CH), BF16), jax.ShapeDtypeStruct((1, TOK, 2 * LANES), BF16)),
        in_specs=[hbm] * 13,
        out_specs=(pl.BlockSpec(memory_space=pltpu.VMEM),) * 2,
        scratch_shapes=[
            V((TOK, CH), BF16), V((TOK, CH), BF16), V((CONV, CH), F32), V((1, CH), F32), V((CH, RANK), BF16),
            V((2 * ST, CH), BF16), V((RANK, CH), BF16), V((1, CH), F32), V((ST, CH), F32), V((1, CH), F32),
            V((TOK, 2 * LANES), BF16), V((1, KEEP), jnp.int32), V((1, KEEP), jnp.int32), V((8, LANES), F32),
            V((16, CH), BF16), V((TOK + 16, CH), F32), V((TOK, CH), BF16), V((TOK, RANK + LANES), F32),
            V((TOK, RANK + LANES), F32), V((16, RANK + LANES), BF16), V((TOK, RANK + LANES), BF16),
            V((TOK * TILES, LANES), F32), V((TOK * TILES, LANES), F32), V((TOK // 8, 8, 2 * ST * LANES), F32),
            V((ST * TILES, LANES), F32), V((ST * TILES, LANES), F32), V((TOK * ST * TILES, LANES), F32),
            V((TOK * TILES, LANES), F32), V((TOK, CH), F32),
            V((TILES, 1, LANES), F32), V((NZ, 1, LANES), F32), V((ST * TILES, LANES), F32), V((ST * TILES, LANES), F32),
            V((1, LANES), F32), V((NX, 1, LANES), F32), V((8, LANES), F32), V((NX, 8, LANES), F32),
            V((ST * TILES, LANES), F32), V((ST * TILES, LANES), F32),
            V((256, LANES), BF16), V((256, LANES), BF16), V((TOK, 2 * LANES), BF16),
            pltpu.SemaphoreType.DMA((14,)),
            pltpu.SemaphoreType.DMA((10,)), pltpu.SemaphoreType.DMA((10,)),
        ],
        compiler_params=pltpu.CompilerParams(
            collective_id=0, has_side_effects=True, vmem_limit_bytes=48 * 1024 * 1024
        ),
    )(
        x_in, gate_in, conv_weight, conv_bias.reshape(1, CH), proj_low, proj_bc.T, dt_weight, dt_bias.reshape(1, CH),
        decay_log, skip_gain.reshape(1, CH), attn_kv, kept_index, kept_owner.reshape(1, KEEP),
    )


def solution(mesh):
    return jax.shard_map(
        local,
        mesh=mesh,
        in_specs=(
            P("ctx", "ch"), P("ctx", "ch"), P(None, "ch"), P("ch"), P("ch", None), P("ch", None), P(None, "ch"),
            P("ch"), P(None, "ch"), P("ch"), P("ctx", "ch"), P("ch", "ctx"), P("ch", "ctx", None),
        ),
        out_specs=(P("ctx", "ch"), P("ch", "ctx", None)),
        check_vma=False,
    )
```

time: 429 us -> 63.2 us (0.15)
  the two profiles are of different devices: /device:TPU:8 before, /device:TPU:2 now
where the time goes in v1:
time: 63.2 us; the launch traced here: 62.7 us
  Pallas kernels  52.1 us (82%)
  local copies, waits for them, and re-layouts  9.91 us (16%)
  between operations  0.69 us (1%)
    pallas_call x1, Pallas kernels, local(): pl.pallas_call(kernel, out_shape=(jax.ShapeDtypeStruct((TOK, CH), BF16),...  52.1 us
    unnamed x28, local copies, waits for them, and re-layouts  9.91 us

profile of v1, /device:TPU:2, one launch (start us, length us, event | category | flops | bytes accessed | tf_op | source)
XLA Modules:
  0.0 62.7 jit_solution(7262121753503708434)
XLA Ops:
  0.6 0.0 copy-start.9
  0.6 0.0 copy-start.8
  0.7 0.0 copy-start.11
  0.7 0.0 copy-start.12
  0.7 0.6 %copy-done.9 = f32[1024]{0:T(1024)S(1)} copy-done((f32[1024]{0:T(1024)S(1)}, f32[1024]{0:T(1024)}, u32[]{:S(2)}) %copy-start.9) | copy-done | bytes 4120
  1.3 0.0 copy-done.8
  1.3 0.0 copy-done.11
  1.3 0.0 copy-done.12
  1.3 0.0 copy-start
  1.3 1.0 %copy-done = bf16[1024,256]{1,0:T(8,128)(2,1)S(1)} copy-done((bf16[1024,256]{1,0:T(8,128)(2,1)S(1)}, bf16[1024,256]{1,0:T(8,128)(2,1)}, u32[]{:S(2)}) %copy-start) | copy-done | bytes 524312
  2.4 0.0 copy-start.1
  2.4 1.0 %copy-done.1 = bf16[256,1024]{1,0:T(8,128)(2,1)S(1)} copy-done((bf16[256,1024]{1,0:T(8,128)(2,1)S(1)}, bf16[256,1024]{1,0:T(8,128)(2,1)}, u32[]{:S(2)}) %copy-start.1) | copy-done | bytes 524312
  3.4 0.0 copy-start.2
  3.4 0.9 %copy-done.2 = bf16[128,1024]{1,0:T(8,128)(2,1)S(1)} copy-done((bf16[128,1024]{1,0:T(8,128)(2,1)S(1)}, bf16[128,1024]{1,0:T(8,128)(2,1)}, u32[]{:S(2)}) %copy-start.2) | copy-done | bytes 262168
  4.4 0.0 copy-start.3
  4.4 0.9 %copy-done.3 = bf16[128,1024]{1,0:T(8,128)(2,1)S(1)} copy-done((bf16[128,1024]{1,0:T(8,128)(2,1)S(1)}, bf16[128,1024]{1,0:T(8,128)(2,1)}, u32[]{:S(2)}) %copy-start.3) | copy-done | bytes 262168
  5.3 0.0 copy-start.4
  5.3 0.8 %copy-done.4 = bf16[1024,32]{0,1:T(8,128)(2,1)S(1)} copy-done((bf16[1024,32]{0,1:T(8,128)(2,1)S(1)}, bf16[1024,32]{0,1:T(8,128)(2,1)}, u32[]{:S(2)}) %copy-start.4) | copy-done | bytes 65560
  6.2 0.0 copy-start.5
  6.2 0.8 %copy-done.5 = f32[16,1024]{1,0:T(8,128)S(1)} copy-done((f32[16,1024]{1,0:T(8,128)S(1)}, f32[16,1024]{1,0:T(8,128)}, u32[]{:S(2)}) %copy-start.5) | copy-done | bytes 65560
  7.0 0.0 copy-start.6
  7.0 0.8 %copy-done.6 = bf16[128,256]{1,0:T(8,128)(2,1)S(1)} copy-done((bf16[128,256]{1,0:T(8,128)(2,1)S(1)}, bf16[128,256]{1,0:T(8,128)(2,1)}, u32[]{:S(2)}) %copy-start.6) | copy-done | bytes 65560
  7.9 0.0 copy-start.7
  7.9 0.7 %copy-done.7 = f32[4,1024]{1,0:T(4,128)S(1)} copy-done((f32[4,1024]{1,0:T(4,128)S(1)}, f32[4,1024]{1,0:T(4,128)}, u32[]{:S(2)}) %copy-start.7) | copy-done | bytes 16408
  8.6 0.0 copy-start.10
  8.6 0.7 %copy-done.10 = f32[1024]{0:T(1024)S(1)} copy-done((f32[1024]{0:T(1024)S(1)}, f32[1024]{0:T(1024)}, u32[]{:S(2)}) %copy-start.10) | copy-done | bytes 4120
  9.3 52.1 %shard_map.140 = (bf16[128,1024]{1,0:T(8,128)(2,1)S(1)}, bf16[1,128,256]{2,1,0:T(8,128)(2,1)S(1)}) custom-call(bf16[128,1024]{1,0:T(8,128)(2,1)S(1)} %copy-done.2, bf16[128,1024]{1,0:T(8,128)(2,1)S(1)} %copy-done.3, f32[4,1024]{1,0:T(4,128)S(1)} %copy-done.7, f32[1,1024]{1,0:T(1,128)S(1)} %bitcast.6, bf16[1024,256]{1,0:T(8,128)(2,1)S(1)} %copy-done, ...), custom_call_target="tpu_custom_call" | custom-call | tf_op jit(solution)/shard_map/pallas_call | solution.py:339
  61.3 0.7 %copy.17 = bf16[128,1024]{1,0:T(8,128)(2,1)} copy(bf16[128,1024]{1,0:T(8,128)(2,1)S(1)} %get-tuple-element.4) | data formatting | bytes 524288
  62.0 0.6 %copy.18 = bf16[1,128,256]{2,1,0:T(8,128)(2,1)} copy(bf16[1,128,256]{2,1,0:T(8,128)(2,1)S(1)} %get-tuple-element.5) | data formatting | bytes 131072
Async XLA Ops:
  0.6 0.7 %copy-start.9 = (f32[1024]{0:T(1024)S(1)}, f32[1024]{0:T(1024)}, u32[]{:S(2)}) copy-start(f32[1024]{0:T(1024)} %param.20) | copy-start | bytes 12292
  0.6 0.7 %copy-start.8 = (f32[1024]{0:T(1024)S(1)}, f32[1024]{0:T(1024)}, u32[]{:S(2)}) copy-start(f32[1024]{0:T(1024)} %param.16) | copy-start | bytes 12292
  0.7 0.7 %copy-start.11 = (s32[1,32]{1,0:T(1,128)S(1)}, s32[1,32]{1,0:T(1,128)}, u32[]{:S(2)}) copy-start(s32[1,32]{1,0:T(1,128)} %idx_hbm.1) | copy-start | bytes 388
  0.7 0.7 %copy-start.12 = (s32[1,32,1]{1,2,0:T(1,128)S(1)}, s32[1,32,1]{1,2,0:T(1,128)}, u32[]{:S(2)}) copy-start(s32[1,32,1]{1,2,0:T(1,128)} %param.25) | copy-start | bytes 388
  1.3 1.0 %copy-start = (bf16[1024,256]{1,0:T(8,128)(2,1)S(1)}, bf16[1024,256]{1,0:T(8,128)(2,1)}, u32[]{:S(2)}) copy-start(bf16[1024,256]{1,0:T(8,128)(2,1)} %low_hbm.1) | copy-start | bytes 1572868
  2.4 1.0 %copy-start.1 = (bf16[256,1024]{1,0:T(8,128)(2,1)S(1)}, bf16[256,1024]{1,0:T(8,128)(2,1)}, u32[]{:S(2)}) copy-start(bf16[256,1024]{1,0:T(8,128)(2,1)} %dtw_hbm.1) | copy-start | bytes 1572868
  3.4 0.9 %copy-start.2 = (bf16[128,1024]{1,0:T(8,128)(2,1)S(1)}, bf16[128,1024]{1,0:T(8,128)(2,1)}, u32[]{:S(2)}) copy-start(bf16[128,1024]{1,0:T(8,128)(2,1)} %x_hbm.1) | copy-start | bytes 786436
  4.4 0.9 %copy-start.3 = (bf16[128,1024]{1,0:T(8,128)(2,1)S(1)}, bf16[128,1024]{1,0:T(8,128)(2,1)}, u32[]{:S(2)}) copy-start(bf16[128,1024]{1,0:T(8,128)(2,1)} %gate_hbm.1) | copy-start | bytes 786436
  5.3 0.8 %copy-start.4 = (bf16[1024,32]{0,1:T(8,128)(2,1)S(1)}, bf16[1024,32]{0,1:T(8,128)(2,1)}, u32[]{:S(2)}) copy-start(bf16[1024,32]{0,1:T(8,128)(2,1)} %param.18) | copy-start | bytes 196612
  6.2 0.8 %copy-start.5 = (f32[16,1024]{1,0:T(8,128)S(1)}, f32[16,1024]{1,0:T(8,128)}, u32[]{:S(2)}) copy-start(f32[16,1024]{1,0:T(8,128)} %dec_hbm.1) | copy-start | bytes 196612
  7.0 0.8 %copy-start.6 = (bf16[128,256]{1,0:T(8,128)(2,1)S(1)}, bf16[128,256]{1,0:T(8,128)(2,1)}, u32[]{:S(2)}) copy-start(bf16[128,256]{1,0:T(8,128)(2,1)} %kv_hbm.1) | copy-start | bytes 196612
  7.9 0.7 %copy-start.7 = (f32[4,1024]{1,0:T(4,128)S(1)}, f32[4,1024]{1,0:T(4,128)}, u32[]{:S(2)}) copy-start(f32[4,1024]{1,0:T(4,128)} %cw_hbm.1) | copy-start | bytes 49156
  8.6 0.7 %copy-start.10 = (f32[1024]{0:T(1024)S(1)}, f32[1024]{0:T(1024)}, u32[]{:S(2)}) copy-start(f32[1024]{0:T(1024)} %param.22) | copy-start | bytes 12292

commit v2 on v1

v2 whole, which is shorter than its diff:
```python
import functools
import math

import jax
import jax.numpy as jnp
from jax import lax
from jax.experimental import pallas as pl
from jax.experimental.pallas import tpu as pltpu
from jax.sharding import PartitionSpec as P

MOST = 2
NZ = 16
NX = 4
NC = 8
TOK = 128
CH = 1024
ST = 16
CONV = 4
RANK = 256
LANES = 128
TILES = CH // LANES
KEEP = 32
F32 = jnp.float32
BF16 = jnp.bfloat16
LOG2E = math.log2(math.e)


def dot(a, b):
    return jnp.dot(a, b, preferred_element_type=F32)


def dot_rows(a, b):
    return lax.dot_general(a, b, (((0,), (0,)), ((), ())), preferred_element_type=F32)


def silu(v):
    return v / (1.0 + jnp.exp(-v))


def iota(shape, dim):
    return lax.broadcasted_iota(jnp.int32, shape, dim)


def kernel(
    x_hbm, gate_hbm, cw_hbm, cb_hbm, low_hbm, bc_hbm, dtw_hbm, dtb_hbm, dec_hbm, skip_hbm, kv_hbm, idx_hbm, own_hbm,
    gated_out, kept_out,
    x_v, gate_v, cw_v, cb_v, low_v, bc_v, dtw_v, dtb_v, dec_v, skip_v, kv_v, idx_v, own_v, decs_v,
    halo, xs, act, part, rs_in, ag_out, lr, dtb3, xb3, bcx, a2b, lb, gb, yb, sg,
    s_out, s_in, l_out, l_in, sx_out, sx_in, t_out, t_in, h_out, h_in, hf, decay, reach, before,
    kz_out, kz_in, kx_out,
    in_sem, send_sem, recv_sem, here_sem,
):
    kx_in = kept_out.at[0]
    me = lax.axis_index("ctx")
    mc = lax.axis_index("ch")
    mx = me // NZ
    mz = me % NZ
    mq = mz % 4

    loads = [
        (x_hbm, x_v), (cw_hbm, cw_v), (cb_hbm, cb_v), (idx_hbm, idx_v), (own_hbm, own_v), (kv_hbm, kv_v),
        (low_hbm, low_v), (bc_hbm, bc_v), (dec_hbm, dec_v),
        (dec_hbm.at[:, pl.ds(pl.multiple_of(mq * 2 * LANES, 2 * LANES), 2 * LANES)], decs_v),
        (dtw_hbm, dtw_v), (dtb_hbm, dtb_v), (skip_hbm, skip_v), (gate_hbm, gate_v),
    ]
    loads = [pltpu.make_async_copy(s, d, in_sem.at[i]) for i, (s, d) in enumerate(loads)]
    (x_ld, cw_ld, cb_ld, idx_ld, own_ld, kv_ld, low_ld, bc_ld, dec_ld, decs_ld, dtw_ld, dtb_ld, skip_ld, gate_ld) = loads

    for c in loads:
        c.start()

    def along_z(d):
        return {"ctx": mx * NZ + (mz + d + NZ) % NZ}

    def along_x(d):
        return {"ctx": ((mx + d) % NX) * NZ + mz}

    def along_ch(dy, dc):
        return {"ch": ((mc // 2 + dy) % (NC // 2)) * 2 + (mc + dc) % 2}

    far_z = (8, 7, 9, 6, 10, 5, 11, 4, 12, 3, 13, 2, 14, 1, 15)
    far_x = (2, 1, 3)
    far_ch = ((2, 0), (2, 1), (1, 0), (3, 0), (1, 1), (3, 1), (0, 1))
    right = {"ctx": (me + 1) % (NX * NZ)}
    left = {"ctx": (me + NX * NZ - 1) % (NX * NZ)}
    barrier = pltpu.get_barrier_semaphore()
    for d in far_ch:
        pl.semaphore_signal(barrier, inc=1, device_id=along_ch(*d))
    for d in (-1, 1):
        pl.semaphore_signal(barrier, inc=1, device_id=along_z(d))
    for d in far_x:
        pl.semaphore_signal(barrier, inc=1, device_id=along_x(d))

    @pl.when(mz == NZ - 1)
    def _():
        pl.semaphore_signal(barrier, inc=1, device_id=right)

    @pl.when(mz == 0)
    def _():
        pl.semaphore_signal(barrier, inc=1, device_id=left)

    pl.semaphore_wait(barrier, NC - 1 + NX - 1 + 2 + jnp.where((mz == 0) | (mz == NZ - 1), 1, 0))

    def tell(i):
        for d in (-(1 << i), 1 << i):
            pl.semaphore_signal(here_sem.at[i], inc=1, device_id=along_z(d))

    def hear(i):
        pl.semaphore_wait(here_sem.at[i], 2)

    def remote(src, dst, k, peer):
        return pltpu.make_async_remote_copy(
            src_ref=src, dst_ref=dst, send_sem=send_sem.at[k], recv_sem=recv_sem.at[k], device_id=peer
        )

    def drain(ref, sem):
        pltpu.make_async_copy(ref, ref, sem).wait()

    HALO, RS, AG, KZ, KX, SZ, LZ, SX, TX, HZ = range(10)

    remote(x_hbm.at[pl.ds(TOK - 16, 16), :], halo, HALO, right).start()
    tell(0)

    x_ld.wait()
    cw_ld.wait()
    cb_ld.wait()
    xs[pl.ds(16, TOK), :] = x_v[...].astype(F32)
    for j in range(TILES):
        cols = pl.ds(j * LANES, LANES)
        s = jnp.broadcast_to(cb_v[:, cols], (TOK - 16, LANES))
        for k in range(CONV):
            s = s + cw_v[pl.ds(k, 1), cols] * xs[pl.ds(32 - (CONV - 1) + k, TOK - 16), cols]
        a = silu(s).astype(BF16)
        act[pl.ds(16, TOK - 16), cols] = a
        xb3[pl.ds(16 * TILES + j, TOK - 16, stride=TILES), :] = a.astype(F32)

    idx_ld.wait()
    own_ld.wait()
    kv_ld.wait()
    own_row = own_v[...]
    eye = iota((KEEP, KEEP), 0) == iota((KEEP, KEEP), 1)
    own = jnp.sum(jnp.where(eye, own_row, 0), axis=1, keepdims=True)
    same = (own_row == own) & (iota((KEEP, KEEP), 1) < iota((KEEP, KEEP), 0))
    rank = jnp.sum(jnp.where(same, 1, 0), axis=1, keepdims=True)
    place = (own & (NZ - 1)) * 16 + (own >> 4) * 2 + rank
    src_t = (iota((TOK, KEEP), 0) == idx_v[...] - me * TOK).astype(F32).astype(BF16)
    picked = dot_rows(src_t, kv_v[...]).astype(BF16)
    slots = iota((KEEP, 256), 1)
    kz = dot_rows((slots == place).astype(F32).astype(BF16), picked[:, :LANES])
    kz = kz + dot_rows((slots == place + 8).astype(F32).astype(BF16), picked[:, LANES:])
    kz_out[...] = kz.astype(BF16)

    hear(0)
    tell(1)
    drain(halo, recv_sem.at[HALO])
    xs[pl.ds(0, 16), :] = jnp.where(me > 0, halo[...].astype(F32), 0.0)
    for j in range(TILES):
        cols = pl.ds(j * LANES, LANES)
        s = jnp.broadcast_to(cb_v[:, cols], (16, LANES))
        for k in range(CONV):
            s = s + cw_v[pl.ds(k, 1), cols] * xs[pl.ds(16 - (CONV - 1) + k, 16), cols]
        a = silu(s).astype(BF16)
        act[pl.ds(0, 16), cols] = a
        xb3[pl.ds(j, 16, stride=TILES), :] = a.astype(F32)

    low_ld.wait()
    bc_ld.wait()
    part[:, pl.ds(RANK, LANES)] = jnp.zeros((TOK, LANES), BF16)
    part[:, pl.ds(0, RANK)] = dot(act[...], low_v[...]).astype(BF16)
    part[:, pl.ds(RANK, 2 * ST)] = lax.dot_general(
        act[...], bc_v[...], (((1,), (1,)), ((), ())), preferred_element_type=F32
    ).astype(BF16)

    def rows_of(i):
        return pl.ds(pl.multiple_of(i * 16, 16), 16)

    for d in far_ch:
        to = along_ch(*d)
        remote(part.at[rows_of(to["ch"]), :], rs_in.at[rows_of(mc), :], RS, to).start()
    rs_in[rows_of(mc), :] = part[rows_of(mc), :]
    hear(1)
    tell(2)

    dec_ld.wait()
    decs_ld.wait()
    gate_ld.wait()
    for j in range(TILES):
        a2b[pl.ds(j, ST, stride=TILES), :] = -LOG2E * jnp.exp(dec_v[:, pl.ds(j * LANES, LANES)])
    a2s = [-LOG2E * jnp.exp(decs_v[:, pl.ds(jj * LANES, LANES)]) for jj in range(2)]
    sg[...] = silu(gate_v[...].astype(F32))

    drain(rs_in.at[pl.ds(0, TOK - 16), :], recv_sem.at[RS])
    total = rs_in[pl.ds(0, 16), :].astype(F32)
    for i in range(1, NC):
        total = total + rs_in[pl.ds(16 * i, 16), :].astype(F32)
    ag_out[...] = total.astype(BF16)
    for d in far_ch:
        remote(ag_out, lr.at[rows_of(mc), :], AG, along_ch(*d)).start()
    lr[rows_of(mc), :] = ag_out[...]
    hear(2)
    for d in far_z:
        to = (mz + d) % NZ
        remote(kz_out.at[rows_of(to), :], kz_in.at[rows_of(mz), :], KZ, along_z(d)).start()
    kz_in[rows_of(mz), :] = kz_out[rows_of(mz), :]

    dtw_ld.wait()
    dtb_ld.wait()
    skip_ld.wait()
    drain(lr.at[pl.ds(0, TOK - 16), :], recv_sem.at[AG])

    for j in range(TILES):
        cols = pl.ds(j * LANES, LANES)
        v = dot(lr[:, pl.ds(0, RANK)], dtw_v[:, cols]) + dtb_v[:, cols]
        dtb3[pl.ds(j, TOK, stride=TILES), :] = jnp.maximum(v, 0.0) + jnp.log1p(jnp.exp(-jnp.abs(v)))
    coeff = lr[:, pl.ds(RANK, LANES)][:, : 2 * ST]

    def spread(i):
        rows = (iota((2 * ST, 4 * LANES), 1) >> 7) + 4 * i == iota((2 * ST, 4 * LANES), 0)
        wide = dot(coeff, rows.astype(F32).astype(BF16))
        bcx[:, :, pl.ds(i * 4 * LANES, 4 * LANES)] = wide.reshape(TOK // 8, 8, 4 * LANES)

    for i in range(4):
        spread(i)

    def token(g, u):
        return pl.ds(pl.multiple_of(g * 64, 64) + u * 8, 8)

    def total_step(g, acc):
        for u in range(8):
            acc = acc + dtb3[token(g, u), :]
        return acc

    s_total = lax.fori_loop(0, TOK // 8, total_step, jnp.zeros((TILES, LANES), F32))
    for j in range(TILES):
        s_out[j] = s_total[j : j + 1, :]
    for d in far_z:
        to = (mz + d) % 4
        remote(s_out.at[pl.ds(2 * to, 2)], s_in.at[mz], SZ, along_z(d)).start()
    s_in[mz] = s_out[pl.ds(2 * mq, 2)]

    def end_step(g, state):
        state = list(state)
        for u in range(8):
            dt = dtb3[token(g, u), :]
            dx = dt * xb3[token(g, u), :]
            for n in range(ST):
                b = bcx[g, pl.ds(u, 1), pl.ds(n * LANES, LANES)]
                state[n] = jnp.exp2(dt * a2b[pl.ds(n * 8, 8), :]) * state[n] + dx * b
        return tuple(state)

    empty = tuple(jnp.zeros((TILES, LANES), F32) for _ in range(ST))
    state = lax.fori_loop(0, TOK // 8, end_step, empty)
    for n in range(ST):
        lb[pl.ds(n * 8, 8), :] = state[n]
    for j in range(TILES):
        l_out[pl.ds(j * ST, ST), :] = lb[pl.ds(j, ST, stride=TILES), :].astype(BF16)

    def block_of(i):
        return pl.ds(pl.multiple_of(i * 32, 32), 32)

    for d in far_z:
        to = (mz + d) % 4
        remote(l_out.at[block_of(to), :], l_in.at[block_of(mz), :], LZ, along_z(d)).start()
    l_in[block_of(mz), :] = l_out[block_of(mq), :]

    for i in range(4, 8):
        spread(i)

    def scan_step(g, state):
        state = list(state)
        for u in range(8):
            dt = dtb3[token(g, u), :]
            dx = dt * xb3[token(g, u), :]
            y = [None] * 4
            for n in range(ST):
                b = bcx[g, pl.ds(u, 1), pl.ds(n * LANES, LANES)]
                c = bcx[g, pl.ds(u, 1), pl.ds((ST + n) * LANES, LANES)]
                state[n] = jnp.exp2(dt * a2b[pl.ds(n * 8, 8), :]) * state[n] + dx * b
                term = c * state[n]
                y[n % 4] = term if y[n % 4] is None else y[n % 4] + term
            yb[token(g, u), :] = (y[0] + y[1]) + (y[2] + y[3])
        return tuple(state)

    lax.fori_loop(0, TOK // 8, scan_step, empty)

    def reach_step(g, cum):
        for u in range(8):
            cum = cum + dtb3[token(g, u), :]
            for n in range(ST):
                c = bcx[g, pl.ds(u, 1), pl.ds((ST + n) * LANES, LANES)]
                gb[pl.ds(pl.multiple_of(g * 1024, 1024) + u * 128 + n * 8, 8), :] = c * jnp.exp2(cum * a2b[pl.ds(n * 8, 8), :])
        return cum

    lax.fori_loop(0, TOK // 8, reach_step, jnp.zeros((TILES, LANES), F32))

    drain(kz_in.at[pl.ds(0, 240), :], recv_sem.at[KZ])
    row = iota((TOK, 256), 0)
    want = ((row >> 1) & (NZ - 1)) * 16 + (row >> 5) * 2 + (row & 1)
    for half in range(2):
        sel = (iota((TOK, 256), 1) == want + half * 8).astype(F32).astype(BF16)
        kx_out[:, pl.ds(half * LANES, LANES)] = dot(sel, kz_in[...]).astype(BF16)

    for d in far_x:
        to = (mx + d) % NX
        remote(kx_out.at[block_of(to), :], kx_in.at[block_of(mx), :], KX, along_x(d)).start()
    kx_in[block_of(mx), :] = kx_out[block_of(mx), :]

    drain(s_in.at[pl.ds(0, NZ - 1)], recv_sem.at[SZ])
    for jj in range(2):
        run = jnp.zeros((1, LANES), F32)
        for z in range(NZ):
            rows = pl.ds(z * 32 + jj * ST, ST)
            decay[rows, :] = jnp.exp2(a2s[jj] * s_in[z, jj])
            reach[rows, :] = jnp.exp2(a2s[jj] * run)
            run = run + s_in[z, jj]
        sx_out[jj] = run
    for d in far_x:
        remote(sx_out, sx_in.at[mx], SX, along_x(d)).start()
    sx_in[mx] = sx_out[...]

    drain(l_in.at[pl.ds(0, 480), :], recv_sem.at[LZ])
    for jj in range(2):
        carry = jnp.zeros((ST, LANES), F32)
        for z in range(NZ):
            rows = pl.ds(z * 32 + jj * ST, ST)
            before[rows, :] = carry
            carry = decay[rows, :] * carry + l_in[rows, :].astype(F32)
        t_out[pl.ds(jj * ST, ST), :] = carry.astype(BF16)
    for d in far_x:
        remote(t_out, t_in.at[mx], TX, along_x(d)).start()
    t_in[mx] = t_out[...]
    drain(sx_in.at[pl.ds(0, NX - 1)], recv_sem.at[SX])
    drain(t_in.at[pl.ds(0, NX - 1)], recv_sem.at[TX])
    plane = []
    for jj in range(2):
        p = jnp.zeros((ST, LANES), F32)
        for i in range(NX - 1):
            later = jnp.exp2(a2s[jj] * sx_in[i, jj]) * p + t_in[i, pl.ds(jj * ST, ST), :].astype(F32)
            p = jnp.where(i < mx, later, p)
        plane.append(p)

    for k, d in enumerate((-2, -1, 1, 0)):
        z = (mz + d + NZ) % NZ
        for jj in range(2):
            rows = pl.ds(pl.multiple_of(z * 32, 32) + jj * ST, ST)
            h_out[pl.ds(k * 32 + jj * ST, ST), :] = (before[rows, :] + reach[rows, :] * plane[jj]).astype(BF16)
        if d:
            remote(h_out.at[pl.ds(k * 32, 32), :], h_in.at[block_of(mq), :], HZ, along_z(d)).start()
    h_in[block_of(mq), :] = h_out[pl.ds(96, 32), :]
    drain(h_in.at[pl.ds(0, 96), :], recv_sem.at[HZ])
    hf[...] = h_in[...].astype(F32)

    carried = [hf[pl.ds(n, TILES, stride=ST), :] for n in range(ST)]

    def add_step(g, _):
        for u in range(8):
            at = token(g, u)
            y = [yb[at, :], None, None, None]
            for n in range(ST):
                term = gb[pl.ds(pl.multiple_of(g * 1024, 1024) + u * 128 + n * 8, 8), :] * carried[n]
                y[n % 4] = term if y[n % 4] is None else y[n % 4] + term
            yb[at, :] = (y[0] + y[1]) + (y[2] + y[3])
        return 0

    lax.fori_loop(0, TOK // 8, add_step, 0)

    for j in range(TILES):
        cols = pl.ds(j * LANES, LANES)
        y = yb[pl.ds(j, TOK, stride=TILES), :] + skip_v[:, cols] * act[:, cols].astype(F32)
        gated_out[:, cols] = (y * sg[:, cols]).astype(BF16)
    drain(kx_in.at[pl.ds(0, 96), :], recv_sem.at[KX])

    drain(halo, send_sem.at[HALO])
    drain(rs_in.at[pl.ds(0, TOK - 16), :], send_sem.at[RS])
    drain(lr.at[pl.ds(0, TOK - 16), :], send_sem.at[AG])
    drain(kz_in.at[pl.ds(0, 240), :], send_sem.at[KZ])
    drain(kx_in.at[pl.ds(0, 96), :], send_sem.at[KX])
    drain(s_in.at[pl.ds(0, NZ - 1)], send_sem.at[SZ])
    drain(l_in.at[pl.ds(0, 480), :], send_sem.at[LZ])
    drain(sx_in.at[pl.ds(0, NX - 1)], send_sem.at[SX])
    drain(t_in.at[pl.ds(0, NX - 1)], send_sem.at[TX])
    drain(h_in.at[pl.ds(0, 96), :], send_sem.at[HZ])


def local(
    x_in, gate_in, conv_weight, conv_bias, proj_low, proj_bc, dt_weight, dt_bias, decay_log, skip_gain, attn_kv,
    kept_index, kept_owner,
):
    V = pltpu.VMEM
    hbm = pl.BlockSpec(memory_space=pltpu.HBM)
    return pl.pallas_call(
        kernel,
        out_shape=(jax.ShapeDtypeStruct((TOK, CH), BF16), jax.ShapeDtypeStruct((1, TOK, 2 * LANES), BF16)),
        in_specs=[hbm] * 13,
        out_specs=(pl.BlockSpec(memory_space=pltpu.VMEM),) * 2,
        scratch_shapes=[
            V((TOK, CH), BF16), V((TOK, CH), BF16), V((CONV, CH), F32), V((1, CH), F32), V((CH, RANK), BF16),
            V((2 * ST, CH), BF16), V((RANK, CH), BF16), V((1, CH), F32), V((ST, CH), F32), V((1, CH), F32),
            V((TOK, 2 * LANES), BF16), V((1, KEEP), jnp.int32), V((1, KEEP), jnp.int32), V((ST, 2 * LANES), F32),
            V((16, CH), BF16), V((TOK + 16, CH), F32), V((TOK, CH), BF16), V((TOK, RANK + LANES), BF16),
            V((TOK, RANK + LANES), BF16), V((16, RANK + LANES), BF16), V((TOK, RANK + LANES), BF16),
            V((TOK * TILES, LANES), F32), V((TOK * TILES, LANES), F32), V((TOK // 8, 8, 2 * ST * LANES), F32),
            V((ST * TILES, LANES), F32), V((ST * TILES, LANES), F32), V((TOK * ST * TILES, LANES), F32),
            V((TOK * TILES, LANES), F32), V((TOK, CH), F32),
            V((TILES, 1, LANES), F32), V((NZ, 2, 1, LANES), F32), V((ST * TILES, LANES), BF16), V((NZ * 32, LANES), BF16),
            V((2, 1, LANES), F32), V((NX, 2, 1, LANES), F32), V((32, LANES), BF16), V((NX, 32, LANES), BF16),
            V((ST * TILES, LANES), BF16), V((ST * TILES, LANES), BF16), V((ST * TILES, LANES), F32),
            V((NZ * 32, LANES), F32), V((NZ * 32, LANES), F32), V((NZ * 32, LANES), F32),
            V((256, LANES), BF16), V((256, LANES), BF16), V((TOK, 2 * LANES), BF16),
            pltpu.SemaphoreType.DMA((14,)),
            pltpu.SemaphoreType.DMA((10,)), pltpu.SemaphoreType.DMA((10,)),
            pltpu.SemaphoreType.REGULAR((3,)),
        ],
        compiler_params=pltpu.CompilerParams(
            collective_id=0, has_side_effects=True, vmem_limit_bytes=62_000_000
        ),
    )(
        x_in, gate_in, conv_weight, conv_bias.reshape(1, CH), proj_low, proj_bc.T, dt_weight, dt_bias.reshape(1, CH),
        decay_log, skip_gain.reshape(1, CH), attn_kv, kept_index, kept_owner.reshape(1, KEEP),
    )


def solution(mesh):
    return jax.shard_map(
        local,
        mesh=mesh,
        in_specs=(
            P("ctx", "ch"), P("ctx", "ch"), P(None, "ch"), P("ch"), P("ch", None), P("ch", None), P(None, "ch"),
            P("ch"), P(None, "ch"), P("ch"), P("ctx", "ch"), P("ch", "ctx"), P("ch", "ctx", None),
        ),
        out_specs=(P("ctx", "ch"), P("ch", "ctx", None)),
        check_vma=False,
    )
```

time: 63.2 us -> 47 us (0.74)
  Pallas kernels: 52.1 us -> 43.8 us
  local copies, waits for them, and re-layouts: 9.91 us -> 2.33 us
    pallas_call x1, Pallas kernels: 52.1 us -> 43.8 us  [local(): pl.pallas_call(kernel, out_shape=(jax.ShapeDtypeStruct((TOK, CH), BF16),...]
    unnamed x28 -> x4, local copies, waits for them, and re-layouts: 9.91 us -> 2.33 us
where the time goes in v2:
time: 47 us; the launch traced here: 46.8 us
  Pallas kernels  43.8 us (93%)
  local copies, waits for them, and re-layouts  2.33 us (5%)
  between operations  0.65 us (1%)
    pallas_call x1, Pallas kernels, local(): pl.pallas_call(kernel, out_shape=(jax.ShapeDtypeStruct((TOK, CH), BF16),...  43.8 us
    unnamed x4, local copies, waits for them, and re-layouts  2.33 us

profile of v2, /device:TPU:2, one launch (start us, length us, event | category | flops | bytes accessed | tf_op | source)
XLA Modules:
  0.0 46.8 jit_solution(8621219483181282946)
XLA Ops:
  0.6 43.8 %shard_map.140 = (bf16[128,1024]{1,0:T(8,128)(2,1)}, bf16[1,128,256]{2,1,0:T(8,128)(2,1)}) custom-call(bf16[128,1024]{1,0:T(8,128)(2,1)} %x_hbm.1, bf16[128,1024]{1,0:T(8,128)(2,1)} %gate_hbm.1, f32[4,1024]{1,0:T(4,128)} %cw_hbm.1, f32[1,1024]{1,0:T(1,128)} %bitcast.6, bf16[1024,256]{1,0:T(8,128)(2,1)} %low_hbm.1, bf16[32,1024]{1,0:T(8,128)(2,1)} %bitcast.5, ...), custom_call_target="tpu_custom_call" | custom-call | tf_op jit(solution)/shard_map/pallas_call | solution.py:391
  44.5 0.0 copy-start
  44.5 1.7 %copy.17 = bf16[128,1024]{1,0:T(8,128)(2,1)} copy(bf16[128,1024]{1,0:T(8,128)(2,1)} %get-tuple-element.4) | data formatting | bytes 524288
  46.2 0.0 copy-done
  46.2 0.6 %copy.18 = bf16[1,128,256]{2,1,0:T(8,128)(2,1)} copy(bf16[1,128,256]{2,1,0:T(8,128)(2,1)S(1)} %copy-done) | data formatting | bytes 131072
Async XLA Ops:
  44.5 1.7 %copy-start = (bf16[1,128,256]{2,1,0:T(8,128)(2,1)S(1)}, bf16[1,128,256]{2,1,0:T(8,128)(2,1)}, u32[]{:S(2)}) copy-start(bf16[1,128,256]{2,1,0:T(8,128)(2,1)} %get-tuple-element.5) | copy-start | bytes 196612

commit v3 on v2

--- a/solution.py
+++ b/solution.py
@@ -45,7 +45,7 @@
     x_hbm, gate_hbm, cw_hbm, cb_hbm, low_hbm, bc_hbm, dtw_hbm, dtb_hbm, dec_hbm, skip_hbm, kv_hbm, idx_hbm, own_hbm,
     gated_out, kept_out,
     x_v, gate_v, cw_v, cb_v, low_v, bc_v, dtw_v, dtb_v, dec_v, skip_v, kv_v, idx_v, own_v, decs_v,
-    halo, xs, act, part, rs_in, ag_out, lr, dtb3, xb3, bcx, a2b, lb, gb, yb, sg,
+    halo, halo_out, halo_f, xs, act, part, rs_in, r0_in, ag_out, lr, dtb3, xb3, bcx, a2b, lb, gb, yb, sg,
     s_out, s_in, l_out, l_in, sx_out, sx_in, t_out, t_in, h_out, h_in, hf, decay, reach, before,
     kz_out, kz_in, kx_out,
     in_sem, send_sem, recv_sem, here_sem,
@@ -59,12 +59,13 @@
 
     loads = [
         (x_hbm, x_v), (cw_hbm, cw_v), (cb_hbm, cb_v), (idx_hbm, idx_v), (own_hbm, own_v), (kv_hbm, kv_v),
-        (low_hbm, low_v), (bc_hbm, bc_v), (dec_hbm, dec_v),
+        (low_hbm, low_v), (bc_hbm, bc_v.at[pl.ds(0, 2 * ST), :]), (bc_hbm, bc_v.at[pl.ds(2 * ST, 2 * ST), :]),
+        (dec_hbm, dec_v),
         (dec_hbm.at[:, pl.ds(pl.multiple_of(mq * 2 * LANES, 2 * LANES), 2 * LANES)], decs_v),
         (dtw_hbm, dtw_v), (dtb_hbm, dtb_v), (skip_hbm, skip_v), (gate_hbm, gate_v),
     ]
     loads = [pltpu.make_async_copy(s, d, in_sem.at[i]) for i, (s, d) in enumerate(loads)]
-    (x_ld, cw_ld, cb_ld, idx_ld, own_ld, kv_ld, low_ld, bc_ld, dec_ld, decs_ld, dtw_ld, dtb_ld, skip_ld, gate_ld) = loads
+    (x_ld, cw_ld, cb_ld, idx_ld, own_ld, kv_ld, low_ld, bc_ld, bc2_ld, dec_ld, decs_ld, dtw_ld, dtb_ld, skip_ld, gate_ld) = loads
 
     for c in loads:
         c.start()
@@ -99,8 +100,6 @@
     def _():
         pl.semaphore_signal(barrier, inc=1, device_id=left)
 
-    pl.semaphore_wait(barrier, NC - 1 + NX - 1 + 2 + jnp.where((mz == 0) | (mz == NZ - 1), 1, 0))
-
     def tell(i):
         for d in (-(1 << i), 1 << i):
             pl.semaphore_signal(here_sem.at[i], inc=1, device_id=along_z(d))
@@ -116,23 +115,74 @@
     def drain(ref, sem):
         pltpu.make_async_copy(ref, ref, sem).wait()
 
-    HALO, RS, AG, KZ, KX, SZ, LZ, SX, TX, HZ = range(10)
-
-    remote(x_hbm.at[pl.ds(TOK - 16, 16), :], halo, HALO, right).start()
+    HALO, RS, AG, KZ, KX, SZ, LZ, SX, TX, HZ, R0 = range(11)
+
+    bc_v[pl.ds(4 * ST, LANES - 4 * ST), :] = jnp.zeros((LANES - 4 * ST, CH), BF16)
+
+    x_ld.wait()
+    for j in range(TILES):
+        halo_f[pl.ds(4 * j, 4), :] = x_v[pl.ds(TOK - 16, 16), pl.ds(j * LANES, LANES)].astype(F32)[12:, :]
+    halo_out[...] = halo_f[...].astype(BF16)
+    pl.semaphore_wait(barrier, NC - 1 + NX - 1 + 2 + jnp.where((mz == 0) | (mz == NZ - 1), 1, 0))
+
+    remote(halo_out, halo, HALO, right).start()
     tell(0)
 
-    x_ld.wait()
+    def conv(first, rows):
+        for j in range(TILES):
+            cols = pl.ds(j * LANES, LANES)
+            s = jnp.broadcast_to(cb_v[:, cols], (rows, LANES))
+            for k in range(CONV):
+                s = s + cw_v[pl.ds(k, 1), cols] * xs[pl.ds(first + 16 - (CONV - 1) + k, rows), cols]
+            a = silu(s).astype(BF16)
+            act[pl.ds(first, rows), cols] = a
+            xb3[pl.ds(first * TILES + j, rows, stride=TILES), :] = a.astype(F32)
+
+    def project(first, rows):
+        a = act[pl.ds(first, rows), :]
+        part[pl.ds(first, rows), pl.ds(0, RANK)] = dot(a, low_v[...]).astype(BF16)
+        wide = lax.dot_general(a, bc_v[...], (((1,), (1,)), ((), ())), preferred_element_type=F32)
+        high = wide.astype(BF16).astype(F32)
+        low = jnp.where(iota((rows, LANES), 1) < 2 * ST, high, wide - high)
+        part[pl.ds(first, rows), pl.ds(RANK, LANES)] = low.astype(BF16)
+
+    def summed(ref):
+        total = ref[pl.ds(0, 16), :].astype(F32)
+        for i in range(1, NC):
+            total = total + ref[pl.ds(16 * i, 16), :].astype(F32)
+        wide = total[:, RANK:]
+        return total[:, :RANK].astype(BF16), (wide + pltpu.roll(wide, LANES - 2 * ST, 1)).astype(BF16)
+
+    def rows_of(i):
+        return pl.ds(pl.multiple_of(i * 16, 16), 16)
+
     cw_ld.wait()
     cb_ld.wait()
     xs[pl.ds(16, TOK), :] = x_v[...].astype(F32)
-    for j in range(TILES):
-        cols = pl.ds(j * LANES, LANES)
-        s = jnp.broadcast_to(cb_v[:, cols], (TOK - 16, LANES))
-        for k in range(CONV):
-            s = s + cw_v[pl.ds(k, 1), cols] * xs[pl.ds(32 - (CONV - 1) + k, TOK - 16), cols]
-        a = silu(s).astype(BF16)
-        act[pl.ds(16, TOK - 16), cols] = a
-        xb3[pl.ds(16 * TILES + j, TOK - 16, stride=TILES), :] = a.astype(F32)
+    conv(16, TOK - 16)
+    low_ld.wait()
+    bc_ld.wait()
+    bc2_ld.wait()
+    project(16, TOK - 16)
+
+    for d in far_ch:
+        to = along_ch(*d)
+
+        @pl.when(to["ch"] > 0)
+        def _():
+            remote(part.at[rows_of(to["ch"]), :], rs_in.at[rows_of(mc), :], RS, to).start()
+
+    hear(0)
+    tell(1)
+    drain(halo, recv_sem.at[HALO])
+    halo_f[...] = halo[...].astype(F32)
+    for j in range(TILES):
+        xs[pl.ds(12, 4), pl.ds(j * LANES, LANES)] = jnp.where(me > 0, halo_f[pl.ds(4 * j, 4), :], 0.0)
+    conv(0, 16)
+    project(0, 16)
+    for d in far_ch:
+        remote(part.at[pl.ds(0, 16), :], r0_in.at[rows_of(mc), :], R0, along_ch(*d)).start()
+    r0_in[rows_of(mc), :] = part[pl.ds(0, 16), :]
 
     idx_ld.wait()
     own_ld.wait()
@@ -150,34 +200,6 @@
     kz = kz + dot_rows((slots == place + 8).astype(F32).astype(BF16), picked[:, LANES:])
     kz_out[...] = kz.astype(BF16)
 
-    hear(0)
-    tell(1)
-    drain(halo, recv_sem.at[HALO])
-    xs[pl.ds(0, 16), :] = jnp.where(me > 0, halo[...].astype(F32), 0.0)
-    for j in range(TILES):
-        cols = pl.ds(j * LANES, LANES)
-        s = jnp.broadcast_to(cb_v[:, cols], (16, LANES))
-        for k in range(CONV):
-            s = s + cw_v[pl.ds(k, 1), cols] * xs[pl.ds(16 - (CONV - 1) + k, 16), cols]
-        a = silu(s).astype(BF16)
-        act[pl.ds(0, 16), cols] = a
-        xb3[pl.ds(j, 16, stride=TILES), :] = a.astype(F32)
-
-    low_ld.wait()
-    bc_ld.wait()
-    part[:, pl.ds(RANK, LANES)] = jnp.zeros((TOK, LANES), BF16)
-    part[:, pl.ds(0, RANK)] = dot(act[...], low_v[...]).astype(BF16)
-    part[:, pl.ds(RANK, 2 * ST)] = lax.dot_general(
-        act[...], bc_v[...], (((1,), (1,)), ((), ())), preferred_element_type=F32
-    ).astype(BF16)
-
-    def rows_of(i):
-        return pl.ds(pl.multiple_of(i * 16, 16), 16)
-
-    for d in far_ch:
-        to = along_ch(*d)
-        remote(part.at[rows_of(to["ch"]), :], rs_in.at[rows_of(mc), :], RS, to).start()
-    rs_in[rows_of(mc), :] = part[rows_of(mc), :]
     hear(1)
     tell(2)
 
@@ -189,14 +211,17 @@
     a2s = [-LOG2E * jnp.exp(decs_v[:, pl.ds(jj * LANES, LANES)]) for jj in range(2)]
     sg[...] = silu(gate_v[...].astype(F32))
 
-    drain(rs_in.at[pl.ds(0, TOK - 16), :], recv_sem.at[RS])
-    total = rs_in[pl.ds(0, 16), :].astype(F32)
-    for i in range(1, NC):
-        total = total + rs_in[pl.ds(16 * i, 16), :].astype(F32)
-    ag_out[...] = total.astype(BF16)
-    for d in far_ch:
-        remote(ag_out, lr.at[rows_of(mc), :], AG, along_ch(*d)).start()
-    lr[rows_of(mc), :] = ag_out[...]
+    @pl.when(mc > 0)
+    def _():
+        rs_in[rows_of(mc), :] = part[rows_of(mc), :]
+        drain(rs_in.at[pl.ds(0, TOK - 16), :], recv_sem.at[RS])
+        low, coeff = summed(rs_in)
+        ag_out[:, pl.ds(0, RANK)] = low
+        ag_out[:, pl.ds(RANK, LANES)] = coeff
+        for d in far_ch:
+            remote(ag_out, lr.at[rows_of(mc), :], AG, along_ch(*d)).start()
+        lr[rows_of(mc), :] = ag_out[...]
+
     hear(2)
     for d in far_z:
         to = (mz + d) % NZ
@@ -206,16 +231,27 @@
     dtw_ld.wait()
     dtb_ld.wait()
     skip_ld.wait()
-    drain(lr.at[pl.ds(0, TOK - 16), :], recv_sem.at[AG])
+    drain(r0_in.at[pl.ds(0, TOK - 16), :], recv_sem.at[R0])
+    low, coeff = summed(r0_in)
+    lr[pl.ds(0, 16), pl.ds(0, RANK)] = low
+    lr[pl.ds(0, 16), pl.ds(RANK, LANES)] = coeff
+
+    @pl.when(mc > 0)
+    def _():
+        drain(lr.at[pl.ds(0, TOK - 32), :], recv_sem.at[AG])
+
+    @pl.when(mc == 0)
+    def _():
+        drain(lr.at[pl.ds(0, TOK - 16), :], recv_sem.at[AG])
 
     for j in range(TILES):
         cols = pl.ds(j * LANES, LANES)
         v = dot(lr[:, pl.ds(0, RANK)], dtw_v[:, cols]) + dtb_v[:, cols]
         dtb3[pl.ds(j, TOK, stride=TILES), :] = jnp.maximum(v, 0.0) + jnp.log1p(jnp.exp(-jnp.abs(v)))
-    coeff = lr[:, pl.ds(RANK, LANES)][:, : 2 * ST]
+    coeff = lr[:, pl.ds(RANK, LANES)]
 
     def spread(i):
-        rows = (iota((2 * ST, 4 * LANES), 1) >> 7) + 4 * i == iota((2 * ST, 4 * LANES), 0)
+        rows = (iota((LANES, 4 * LANES), 1) >> 7) + 4 * i == iota((LANES, 4 * LANES), 0)
         wide = dot(coeff, rows.astype(F32).astype(BF16))
         bcx[:, :, pl.ds(i * 4 * LANES, 4 * LANES)] = wide.reshape(TOK // 8, 8, 4 * LANES)
 
@@ -371,8 +407,17 @@
     drain(kx_in.at[pl.ds(0, 96), :], recv_sem.at[KX])
 
     drain(halo, send_sem.at[HALO])
-    drain(rs_in.at[pl.ds(0, TOK - 16), :], send_sem.at[RS])
-    drain(lr.at[pl.ds(0, TOK - 16), :], send_sem.at[AG])
+    drain(r0_in.at[pl.ds(0, TOK - 16), :], send_sem.at[R0])
+
+    @pl.when(mc > 0)
+    def _():
+        drain(rs_in.at[pl.ds(0, TOK - 32), :], send_sem.at[RS])
+        drain(lr.at[pl.ds(0, TOK - 16), :], send_sem.at[AG])
+
+    @pl.when(mc == 0)
+    def _():
+        drain(rs_in.at[pl.ds(0, TOK - 16), :], send_sem.at[RS])
+
     drain(kz_in.at[pl.ds(0, 240), :], send_sem.at[KZ])
     drain(kx_in.at[pl.ds(0, 96), :], send_sem.at[KX])
     drain(s_in.at[pl.ds(0, NZ - 1)], send_sem.at[SZ])
@@ -390,15 +435,15 @@
     hbm = pl.BlockSpec(memory_space=pltpu.HBM)
     return pl.pallas_call(
         kernel,
-        out_shape=(jax.ShapeDtypeStruct((TOK, CH), BF16), jax.ShapeDtypeStruct((1, TOK, 2 * LANES), BF16)),
+        out_shape=(pltpu.VMEM((TOK, CH), BF16), pltpu.VMEM((1, TOK, 2 * LANES), BF16)),
         in_specs=[hbm] * 13,
         out_specs=(pl.BlockSpec(memory_space=pltpu.VMEM),) * 2,
         scratch_shapes=[
             V((TOK, CH), BF16), V((TOK, CH), BF16), V((CONV, CH), F32), V((1, CH), F32), V((CH, RANK), BF16),
-            V((2 * ST, CH), BF16), V((RANK, CH), BF16), V((1, CH), F32), V((ST, CH), F32), V((1, CH), F32),
+            V((LANES, CH), BF16), V((RANK, CH), BF16), V((1, CH), F32), V((ST, CH), F32), V((1, CH), F32),
             V((TOK, 2 * LANES), BF16), V((1, KEEP), jnp.int32), V((1, KEEP), jnp.int32), V((ST, 2 * LANES), F32),
-            V((16, CH), BF16), V((TOK + 16, CH), F32), V((TOK, CH), BF16), V((TOK, RANK + LANES), BF16),
-            V((TOK, RANK + LANES), BF16), V((16, RANK + LANES), BF16), V((TOK, RANK + LANES), BF16),
+            V((32, LANES), BF16), V((32, LANES), BF16), V((32, LANES), F32), V((TOK + 16, CH), F32), V((TOK, CH), BF16),
+            V((TOK, RANK + LANES), BF16), V((TOK, RANK + LANES), BF16), V((TOK, RANK + LANES), BF16), V((16, RANK + LANES), BF16), V((TOK, RANK + LANES), BF16),
             V((TOK * TILES, LANES), F32), V((TOK * TILES, LANES), F32), V((TOK // 8, 8, 2 * ST * LANES), F32),
             V((ST * TILES, LANES), F32), V((ST * TILES, LANES), F32), V((TOK * ST * TILES, LANES), F32),
             V((TOK * TILES, LANES), F32), V((TOK, CH), F32),
@@ -407,8 +452,8 @@
             V((ST * TILES, LANES), BF16), V((ST * TILES, LANES), BF16), V((ST * TILES, LANES), F32),
             V((NZ * 32, LANES), F32), V((NZ * 32, LANES), F32), V((NZ * 32, LANES), F32),
             V((256, LANES), BF16), V((256, LANES), BF16), V((TOK, 2 * LANES), BF16),
-            pltpu.SemaphoreType.DMA((14,)),
-            pltpu.SemaphoreType.DMA((10,)), pltpu.SemaphoreType.DMA((10,)),
+            pltpu.SemaphoreType.DMA((15,)),
+            pltpu.SemaphoreType.DMA((11,)), pltpu.SemaphoreType.DMA((11,)),
             pltpu.SemaphoreType.REGULAR((3,)),
         ],
         compiler_params=pltpu.CompilerParams(

time: 47 us -> 42.7 us (0.909)
  Pallas kernels: 43.8 us -> 40.5 us
  local copies, waits for them, and re-layouts: 2.33 us -> 1.33 us
    pallas_call x1, Pallas kernels: 43.8 us -> 40.5 us  [local(): pl.pallas_call(kernel, out_shape=(pltpu.VMEM((TOK, CH), BF16), pltpu.VMEM...]
    unnamed x4 -> x2, local copies, waits for them, and re-layouts: 2.33 us -> 1.33 us
where the time goes in v3:
time: 42.7 us; the launch traced here: 42.5 us
  Pallas kernels  40.5 us (95%)
  local copies, waits for them, and re-layouts  1.33 us (3%)
  between operations  0.64 us (1%)
    pallas_call x1, Pallas kernels, local(): pl.pallas_call(kernel, out_shape=(pltpu.VMEM((TOK, CH), BF16), pltpu.VMEM...  40.5 us
    unnamed x2, local copies, waits for them, and re-layouts  1.33 us

profile of v3, /device:TPU:2, one launch (start us, length us, event | category | flops | bytes accessed | tf_op | source)
XLA Modules:
  0.0 42.5 jit_solution(14739419738055082554)
XLA Ops:
  0.6 40.5 %shard_map.140 = (bf16[128,1024]{1,0:T(8,128)(2,1)S(1)}, bf16[1,128,256]{2,1,0:T(8,128)(2,1)S(1)}) custom-call(bf16[128,1024]{1,0:T(8,128)(2,1)} %x_hbm.1, bf16[128,1024]{1,0:T(8,128)(2,1)} %gate_hbm.1, f32[4,1024]{1,0:T(4,128)} %cw_hbm.1, f32[1,1024]{1,0:T(1,128)} %bitcast.6, bf16[1024,256]{1,0:T(8,128)(2,1)} %low_hbm.1, bf16[32,1024]{1,0:T(8,128)(2,1)} %bitcast.5, ...), custom_call_target="tpu_custom_call" | custom-call | tf_op jit(solution)/shard_map/pallas_call | solution.py:436
  41.1 0.7 %copy.17 = bf16[128,1024]{1,0:T(8,128)(2,1)} copy(bf16[128,1024]{1,0:T(8,128)(2,1)S(1)} %get-tuple-element.2) | data formatting | bytes 524288
  41.8 0.6 %copy.18 = bf16[1,128,256]{2,1,0:T(8,128)(2,1)} copy(bf16[1,128,256]{2,1,0:T(8,128)(2,1)S(1)} %get-tuple-element.3) | data formatting | bytes 131072

commit v4 on v3

--- a/solution.py
+++ b/solution.py
@@ -45,8 +45,9 @@
     x_hbm, gate_hbm, cw_hbm, cb_hbm, low_hbm, bc_hbm, dtw_hbm, dtb_hbm, dec_hbm, skip_hbm, kv_hbm, idx_hbm, own_hbm,
     gated_out, kept_out,
     x_v, gate_v, cw_v, cb_v, low_v, bc_v, dtw_v, dtb_v, dec_v, skip_v, kv_v, idx_v, own_v, decs_v,
-    halo, halo_out, halo_f, xs, act, part, rs_in, r0_in, ag_out, lr, dtb3, xb3, bcx, a2b, lb, gb, yb, sg,
-    s_out, s_in, l_out, l_in, sx_out, sx_in, t_out, t_in, h_out, h_in, hf, decay, reach, before,
+    halo, halo_out, halo_f, xs, act, part, rs_in, r0_in, ag_out, lr, dtb3, xb3, bcx, a2b, a2n, lb, gb, yb, sgb, skip_b,
+    s_out, s_in, l_out, l_in, sx_out, sx_in, cum_out, cum_in, t_out, t_in, before, h_in, hf, decay, reach,
+    plane, carry_x,
     kz_out, kz_in, kx_out,
     in_sem, send_sem, recv_sem, here_sem,
 ):
@@ -75,6 +76,9 @@
 
     def along_x(d):
         return {"ctx": ((mx + d) % NX) * NZ + mz}
+
+    def along_xz(dx, dz):
+        return {"ctx": ((mx + dx) % NX) * NZ + (mz + dz + NZ) % NZ}
 
     def along_ch(dy, dc):
         return {"ch": ((mc // 2 + dy) % (NC // 2)) * 2 + (mc + dc) % 2}
@@ -107,6 +111,13 @@
     def hear(i):
         pl.semaphore_wait(here_sem.at[i], 2)
 
+    def tell_x():
+        for d in far_x:
+            pl.semaphore_signal(here_sem.at[3], inc=1, device_id=along_x(d))
+
+    def hear_x():
+        pl.semaphore_wait(here_sem.at[3], NX - 1)
+
     def remote(src, dst, k, peer):
         return pltpu.make_async_remote_copy(
             src_ref=src, dst_ref=dst, send_sem=send_sem.at[k], recv_sem=recv_sem.at[k], device_id=peer
@@ -115,7 +126,7 @@
     def drain(ref, sem):
         pltpu.make_async_copy(ref, ref, sem).wait()
 
-    HALO, RS, AG, KZ, KX, SZ, LZ, SX, TX, HZ, R0 = range(11)
+    HALO, RS, AG, KZ, KX, SZ, LZ, CZ, HZ, R0, CX, TX = (0, 1, 2, 3, 4, 5, 6, 7, 8, 9, 10, 13)
 
     bc_v[pl.ds(4 * ST, LANES - 4 * ST), :] = jnp.zeros((LANES - 4 * ST, CH), BF16)
 
@@ -174,6 +185,7 @@
 
     hear(0)
     tell(1)
+    tell_x()
     drain(halo, recv_sem.at[HALO])
     halo_f[...] = halo[...].astype(F32)
     for j in range(TILES):
@@ -207,9 +219,15 @@
     decs_ld.wait()
     gate_ld.wait()
     for j in range(TILES):
-        a2b[pl.ds(j, ST, stride=TILES), :] = -LOG2E * jnp.exp(dec_v[:, pl.ds(j * LANES, LANES)])
+        rate = -LOG2E * jnp.exp(dec_v[:, pl.ds(j * LANES, LANES)])
+        a2n[pl.ds(j * ST, ST), :] = rate
+        a2b[pl.ds(j, ST, stride=TILES), :] = rate
     a2s = [-LOG2E * jnp.exp(decs_v[:, pl.ds(jj * LANES, LANES)]) for jj in range(2)]
-    sg[...] = silu(gate_v[...].astype(F32))
+    skip_ld.wait()
+    for j in range(TILES):
+        cols = pl.ds(j * LANES, LANES)
+        sgb[pl.ds(j, TOK, stride=TILES), :] = silu(gate_v[:, cols].astype(F32))
+        skip_b[pl.ds(j, 1), :] = skip_v[:, cols]
 
     @pl.when(mc > 0)
     def _():
@@ -223,6 +241,7 @@
         lr[rows_of(mc), :] = ag_out[...]
 
     hear(2)
+    hear_x()
     for d in far_z:
         to = (mz + d) % NZ
         remote(kz_out.at[rows_of(to), :], kz_in.at[rows_of(mz), :], KZ, along_z(d)).start()
@@ -230,7 +249,6 @@
 
     dtw_ld.wait()
     dtb_ld.wait()
-    skip_ld.wait()
     drain(r0_in.at[pl.ds(0, TOK - 16), :], recv_sem.at[R0])
     low, coeff = summed(r0_in)
     lr[pl.ds(0, 16), pl.ds(0, RANK)] = low
@@ -306,15 +324,16 @@
         state = list(state)
         for u in range(8):
             dt = dtb3[token(g, u), :]
-            dx = dt * xb3[token(g, u), :]
-            y = [None] * 4
+            xt = xb3[token(g, u), :]
+            dx = dt * xt
+            y = [skip_b[...] * xt, None, None, None]
             for n in range(ST):
                 b = bcx[g, pl.ds(u, 1), pl.ds(n * LANES, LANES)]
                 c = bcx[g, pl.ds(u, 1), pl.ds((ST + n) * LANES, LANES)]
                 state[n] = jnp.exp2(dt * a2b[pl.ds(n * 8, 8), :]) * state[n] + dx * b
                 term = c * state[n]
                 y[n % 4] = term if y[n % 4] is None else y[n % 4] + term
-            yb[token(g, u), :] = (y[0] + y[1]) + (y[2] + y[3])
+            yb[token(g, u), :] = ((y[0] + y[1]) + (y[2] + y[3])) * sgb[token(g, u), :]
         return tuple(state)
 
     lax.fori_loop(0, TOK // 8, scan_step, empty)
@@ -322,9 +341,10 @@
     def reach_step(g, cum):
         for u in range(8):
             cum = cum + dtb3[token(g, u), :]
+            sgt = sgb[token(g, u), :]
             for n in range(ST):
                 c = bcx[g, pl.ds(u, 1), pl.ds((ST + n) * LANES, LANES)]
-                gb[pl.ds(pl.multiple_of(g * 1024, 1024) + u * 128 + n * 8, 8), :] = c * jnp.exp2(cum * a2b[pl.ds(n * 8, 8), :])
+                gb[pl.ds(pl.multiple_of(g * 1024, 1024) + u * 128 + n * 8, 8), :] = (c * sgt) * jnp.exp2(cum * a2b[pl.ds(n * 8, 8), :])
         return cum
 
     lax.fori_loop(0, TOK // 8, reach_step, jnp.zeros((TILES, LANES), F32))
@@ -345,46 +365,73 @@
     for jj in range(2):
         run = jnp.zeros((1, LANES), F32)
         for z in range(NZ):
-            rows = pl.ds(z * 32 + jj * ST, ST)
-            decay[rows, :] = jnp.exp2(a2s[jj] * s_in[z, jj])
-            reach[rows, :] = jnp.exp2(a2s[jj] * run)
+            decay[pl.ds(z * 32 + jj * ST, ST), :] = jnp.exp2(a2s[jj] * s_in[z, jj])
+            cum_out[z, jj] = run
             run = run + s_in[z, jj]
         sx_out[jj] = run
-    for d in far_x:
-        remote(sx_out, sx_in.at[mx], SX, along_x(d)).start()
-    sx_in[mx] = sx_out[...]
+
+    def pair_of(i):
+        return pl.ds(2 * i, 2)
+
+    def to_planes(src, dst, k):
+        for dx in (3, 2, 1):
+
+            @pl.when(mx + dx < NX)
+            def _():
+                for dz in (-2, -1, 1, 0):
+                    pltpu.make_async_remote_copy(
+                        src_ref=src, dst_ref=dst, send_sem=send_sem.at[k + dx - 1], recv_sem=recv_sem.at[k + mx],
+                        device_id=along_xz(dx, dz),
+                    ).start()
+
+    @pl.when(mx < NX - 1)
+    def _():
+        to_planes(sx_out, sx_in.at[mx, pair_of(mq)], CX)
+
+    for dz in (-2, -1, 1):
+        remote(cum_out.at[(mz + dz + NZ) % NZ], cum_in.at[pair_of(mq)], CZ, along_z(dz)).start()
+    cum_in[pair_of(mq)] = cum_out[mz]
 
     drain(l_in.at[pl.ds(0, 480), :], recv_sem.at[LZ])
     for jj in range(2):
         carry = jnp.zeros((ST, LANES), F32)
         for z in range(NZ):
             rows = pl.ds(z * 32 + jj * ST, ST)
-            before[rows, :] = carry
+            before[rows, :] = carry.astype(BF16)
             carry = decay[rows, :] * carry + l_in[rows, :].astype(F32)
         t_out[pl.ds(jj * ST, ST), :] = carry.astype(BF16)
-    for d in far_x:
-        remote(t_out, t_in.at[mx], TX, along_x(d)).start()
-    t_in[mx] = t_out[...]
-    drain(sx_in.at[pl.ds(0, NX - 1)], recv_sem.at[SX])
-    drain(t_in.at[pl.ds(0, NX - 1)], recv_sem.at[TX])
-    plane = []
-    for jj in range(2):
-        p = jnp.zeros((ST, LANES), F32)
-        for i in range(NX - 1):
-            later = jnp.exp2(a2s[jj] * sx_in[i, jj]) * p + t_in[i, pl.ds(jj * ST, ST), :].astype(F32)
-            p = jnp.where(i < mx, later, p)
-        plane.append(p)
-
-    for k, d in enumerate((-2, -1, 1, 0)):
-        z = (mz + d + NZ) % NZ
-        for jj in range(2):
-            rows = pl.ds(pl.multiple_of(z * 32, 32) + jj * ST, ST)
-            h_out[pl.ds(k * 32 + jj * ST, ST), :] = (before[rows, :] + reach[rows, :] * plane[jj]).astype(BF16)
-        if d:
-            remote(h_out.at[pl.ds(k * 32, 32), :], h_in.at[block_of(mq), :], HZ, along_z(d)).start()
-    h_in[block_of(mq), :] = h_out[pl.ds(96, 32), :]
+
+    @pl.when(mx < NX - 1)
+    def _():
+        to_planes(t_out, t_in.at[mx, block_of(mq)], TX)
+
+    for dz in (-2, -1, 1):
+        remote(before.at[block_of((mz + dz + NZ) % NZ), :], h_in.at[block_of(mq), :], HZ, along_z(dz)).start()
+    h_in[block_of(mq), :] = before[block_of(mz), :]
+
+    carry_x[...] = jnp.zeros_like(carry_x)
+    for i in range(NX - 1):
+
+        @pl.when(i < mx)
+        def _():
+            drain(sx_in.at[i], recv_sem.at[CX + i])
+            for j in range(TILES):
+                rows = pl.ds(j * ST, ST)
+                plane[pl.ds(i * 128 + j * ST, ST), :] = jnp.exp2(a2n[rows, :] * sx_in[i, j])
+
+    drain(cum_in.at[pl.ds(0, 6)], recv_sem.at[CZ])
+    for j in range(TILES):
+        rows = pl.ds(j * ST, ST)
+        reach[rows, :] = jnp.exp2(a2n[rows, :] * cum_in[j])
+    for i in range(NX - 1):
+
+        @pl.when(i < mx)
+        def _():
+            drain(t_in.at[i], recv_sem.at[TX + i])
+            carry_x[...] = plane[pl.ds(i * 128, 128), :] * carry_x[...] + t_in[i].astype(F32)
+
     drain(h_in.at[pl.ds(0, 96), :], recv_sem.at[HZ])
-    hf[...] = h_in[...].astype(F32)
+    hf[...] = h_in[...].astype(F32) + reach[...] * carry_x[...]
 
     carried = [hf[pl.ds(n, TILES, stride=ST), :] for n in range(ST)]
 
@@ -402,8 +449,7 @@
 
     for j in range(TILES):
         cols = pl.ds(j * LANES, LANES)
-        y = yb[pl.ds(j, TOK, stride=TILES), :] + skip_v[:, cols] * act[:, cols].astype(F32)
-        gated_out[:, cols] = (y * sg[:, cols]).astype(BF16)
+        gated_out[:, cols] = yb[pl.ds(j, TOK, stride=TILES), :].astype(BF16)
     drain(kx_in.at[pl.ds(0, 96), :], recv_sem.at[KX])
 
     drain(halo, send_sem.at[HALO])
@@ -422,8 +468,14 @@
     drain(kx_in.at[pl.ds(0, 96), :], send_sem.at[KX])
     drain(s_in.at[pl.ds(0, NZ - 1)], send_sem.at[SZ])
     drain(l_in.at[pl.ds(0, 480), :], send_sem.at[LZ])
-    drain(sx_in.at[pl.ds(0, NX - 1)], send_sem.at[SX])
-    drain(t_in.at[pl.ds(0, NX - 1)], send_sem.at[TX])
+    for dx in (1, 2, 3):
+
+        @pl.when(mx + dx < NX)
+        def _():
+            drain(sx_in.at[0], send_sem.at[CX + dx - 1])
+            drain(t_in.at[0], send_sem.at[TX + dx - 1])
+
+    drain(cum_in.at[pl.ds(0, 6)], send_sem.at[CZ])
     drain(h_in.at[pl.ds(0, 96), :], send_sem.at[HZ])
 
 
@@ -445,16 +497,17 @@
             V((32, LANES), BF16), V((32, LANES), BF16), V((32, LANES), F32), V((TOK + 16, CH), F32), V((TOK, CH), BF16),
             V((TOK, RANK + LANES), BF16), V((TOK, RANK + LANES), BF16), V((TOK, RANK + LANES), BF16), V((16, RANK + LANES), BF16), V((TOK, RANK + LANES), BF16),
             V((TOK * TILES, LANES), F32), V((TOK * TILES, LANES), F32), V((TOK // 8, 8, 2 * ST * LANES), F32),
-            V((ST * TILES, LANES), F32), V((ST * TILES, LANES), F32), V((TOK * ST * TILES, LANES), F32),
-            V((TOK * TILES, LANES), F32), V((TOK, CH), F32),
+            V((ST * TILES, LANES), F32), V((ST * TILES, LANES), F32), V((ST * TILES, LANES), F32),
+            V((TOK * ST * TILES, LANES), F32), V((TOK * TILES, LANES), F32), V((TOK * TILES, LANES), F32), V((TILES, LANES), F32),
             V((TILES, 1, LANES), F32), V((NZ, 2, 1, LANES), F32), V((ST * TILES, LANES), BF16), V((NZ * 32, LANES), BF16),
-            V((2, 1, LANES), F32), V((NX, 2, 1, LANES), F32), V((32, LANES), BF16), V((NX, 32, LANES), BF16),
-            V((ST * TILES, LANES), BF16), V((ST * TILES, LANES), BF16), V((ST * TILES, LANES), F32),
-            V((NZ * 32, LANES), F32), V((NZ * 32, LANES), F32), V((NZ * 32, LANES), F32),
+            V((2, 1, LANES), F32), V((NX - 1, TILES, 1, LANES), F32), V((NZ, 2, 1, LANES), F32), V((TILES, 1, LANES), F32),
+            V((32, LANES), BF16), V((NX - 1, 128, LANES), BF16), V((NZ * 32, LANES), BF16), V((128, LANES), BF16),
+            V((128, LANES), F32), V((NZ * 32, LANES), F32), V((128, LANES), F32), V(((NX - 1) * 128, LANES), F32),
+            V((128, LANES), F32),
             V((256, LANES), BF16), V((256, LANES), BF16), V((TOK, 2 * LANES), BF16),
             pltpu.SemaphoreType.DMA((15,)),
-            pltpu.SemaphoreType.DMA((11,)), pltpu.SemaphoreType.DMA((11,)),
-            pltpu.SemaphoreType.REGULAR((3,)),
+            pltpu.SemaphoreType.DMA((16,)), pltpu.SemaphoreType.DMA((16,)),
+            pltpu.SemaphoreType.REGULAR((4,)),
         ],
         compiler_params=pltpu.CompilerParams(
             collective_id=0, has_side_effects=True, vmem_limit_bytes=62_000_000

time: 42.7 us -> 40.4 us (0.946)
  Pallas kernels: 40.5 us -> 38.3 us
    pallas_call x1, Pallas kernels: 40.5 us -> 38.3 us  [local(): pl.pallas_call(kernel, out_shape=(pltpu.VMEM((TOK, CH), BF16), pltpu.VMEM...]
where the time goes in v4:
time: 40.4 us; the launch traced here: 40.2 us
  Pallas kernels  38.3 us (95%)
  local copies, waits for them, and re-layouts  1.33 us (3%)
  between operations  0.64 us (2%)
    pallas_call x1, Pallas kernels, local(): pl.pallas_call(kernel, out_shape=(pltpu.VMEM((TOK, CH), BF16), pltpu.VMEM...  38.3 us
    unnamed x2, local copies, waits for them, and re-layouts  1.33 us

profile of v4, /device:TPU:2, one launch (start us, length us, event | category | flops | bytes accessed | tf_op | source)
XLA Modules:
  0.0 40.2 jit_solution(10152879737290485918)
XLA Ops:
  0.6 38.3 %shard_map.140 = (bf16[128,1024]{1,0:T(8,128)(2,1)S(1)}, bf16[1,128,256]{2,1,0:T(8,128)(2,1)S(1)}) custom-call(bf16[128,1024]{1,0:T(8,128)(2,1)} %x_hbm.1, bf16[128,1024]{1,0:T(8,128)(2,1)} %gate_hbm.1, f32[4,1024]{1,0:T(4,128)} %cw_hbm.1, f32[1,1024]{1,0:T(1,128)} %bitcast.6, bf16[1024,256]{1,0:T(8,128)(2,1)} %low_hbm.1, bf16[32,1024]{1,0:T(8,128)(2,1)} %bitcast.5, ...), custom_call_target="tpu_custom_call" | custom-call | tf_op jit(solution)/shard_map/pallas_call | solution.py:488
  38.9 0.7 %copy.17 = bf16[128,1024]{1,0:T(8,128)(2,1)} copy(bf16[128,1024]{1,0:T(8,128)(2,1)S(1)} %get-tuple-element.2) | data formatting | bytes 524288
  39.6 0.6 %copy.18 = bf16[1,128,256]{2,1,0:T(8,128)(2,1)} copy(bf16[1,128,256]{2,1,0:T(8,128)(2,1)S(1)} %get-tuple-element.3) | data formatting | bytes 131072

commit v5 on v4

--- a/solution.py
+++ b/solution.py
@@ -68,7 +68,7 @@
     loads = [pltpu.make_async_copy(s, d, in_sem.at[i]) for i, (s, d) in enumerate(loads)]
     (x_ld, cw_ld, cb_ld, idx_ld, own_ld, kv_ld, low_ld, bc_ld, bc2_ld, dec_ld, decs_ld, dtw_ld, dtb_ld, skip_ld, gate_ld) = loads
 
-    for c in loads:
+    for c in loads[:3]:
         c.start()
 
     def along_z(d):
@@ -104,6 +104,9 @@
     def _():
         pl.semaphore_signal(barrier, inc=1, device_id=left)
 
+    for c in loads[3:]:
+        c.start()
+
     def tell(i):
         for d in (-(1 << i), 1 << i):
             pl.semaphore_signal(here_sem.at[i], inc=1, device_id=along_z(d))
@@ -126,7 +129,7 @@
     def drain(ref, sem):
         pltpu.make_async_copy(ref, ref, sem).wait()
 
-    HALO, RS, AG, KZ, KX, SZ, LZ, CZ, HZ, R0, CX, TX = (0, 1, 2, 3, 4, 5, 6, 7, 8, 9, 10, 13)
+    HALO, RS, AG, KZ, KX, SZ, R0, CZ, LZ, HZ, CX, TX = (0, 1, 2, 3, 4, 5, 6, 7, 8, 10, 12, 15)
 
     bc_v[pl.ds(4 * ST, LANES - 4 * ST), :] = jnp.zeros((LANES - 4 * ST, CH), BF16)
 
@@ -220,9 +223,12 @@
     gate_ld.wait()
     for j in range(TILES):
         rate = -LOG2E * jnp.exp(dec_v[:, pl.ds(j * LANES, LANES)])
-        a2n[pl.ds(j * ST, ST), :] = rate
+        for half in range(2):
+            a2n[pl.ds(half * 64 + j * 8, 8), :] = rate[half * 8 : half * 8 + 8, :]
         a2b[pl.ds(j, ST, stride=TILES), :] = rate
-    a2s = [-LOG2E * jnp.exp(decs_v[:, pl.ds(jj * LANES, LANES)]) for jj in range(2)]
+    a2s = [
+        [-LOG2E * jnp.exp(decs_v[pl.ds(half * 8, 8), pl.ds(jj * LANES, LANES)]) for jj in range(2)] for half in range(2)
+    ]
     skip_ld.wait()
     for j in range(TILES):
         cols = pl.ds(j * LANES, LANES)
@@ -265,7 +271,9 @@
     for j in range(TILES):
         cols = pl.ds(j * LANES, LANES)
         v = dot(lr[:, pl.ds(0, RANK)], dtw_v[:, cols]) + dtb_v[:, cols]
-        dtb3[pl.ds(j, TOK, stride=TILES), :] = jnp.maximum(v, 0.0) + jnp.log1p(jnp.exp(-jnp.abs(v)))
+        v = jnp.maximum(v, 0.0) + jnp.log1p(jnp.exp(-jnp.abs(v)))
+        dtb3[pl.ds(j, TOK, stride=TILES), :] = v
+        s_out[j] = jnp.sum(v, axis=0, keepdims=True)
     coeff = lr[:, pl.ds(RANK, LANES)]
 
     def spread(i):
@@ -279,43 +287,45 @@
     def token(g, u):
         return pl.ds(pl.multiple_of(g * 64, 64) + u * 8, 8)
 
-    def total_step(g, acc):
-        for u in range(8):
-            acc = acc + dtb3[token(g, u), :]
-        return acc
-
-    s_total = lax.fori_loop(0, TOK // 8, total_step, jnp.zeros((TILES, LANES), F32))
-    for j in range(TILES):
-        s_out[j] = s_total[j : j + 1, :]
     for d in far_z:
         to = (mz + d) % 4
         remote(s_out.at[pl.ds(2 * to, 2)], s_in.at[mz], SZ, along_z(d)).start()
     s_in[mz] = s_out[pl.ds(2 * mq, 2)]
 
-    def end_step(g, state):
-        state = list(state)
-        for u in range(8):
-            dt = dtb3[token(g, u), :]
-            dx = dt * xb3[token(g, u), :]
-            for n in range(ST):
-                b = bcx[g, pl.ds(u, 1), pl.ds(n * LANES, LANES)]
-                state[n] = jnp.exp2(dt * a2b[pl.ds(n * 8, 8), :]) * state[n] + dx * b
-        return tuple(state)
-
-    empty = tuple(jnp.zeros((TILES, LANES), F32) for _ in range(ST))
-    state = lax.fori_loop(0, TOK // 8, end_step, empty)
-    for n in range(ST):
-        lb[pl.ds(n * 8, 8), :] = state[n]
-    for j in range(TILES):
-        l_out[pl.ds(j * ST, ST), :] = lb[pl.ds(j, ST, stride=TILES), :].astype(BF16)
+    def quarter_of(i):
+        return pl.ds(pl.multiple_of(i * 16, 16), 16)
 
     def block_of(i):
         return pl.ds(pl.multiple_of(i * 32, 32), 32)
 
-    for d in far_z:
-        to = (mz + d) % 4
-        remote(l_out.at[block_of(to), :], l_in.at[block_of(mz), :], LZ, along_z(d)).start()
-    l_in[block_of(mz), :] = l_out[block_of(mq), :]
+    empty = tuple(jnp.zeros((TILES, LANES), F32) for _ in range(ST))
+
+    def half_block(half, i):
+        return pl.ds(half * 64 + pl.multiple_of(i * 16, 16), 16)
+
+    for half in range(2):
+
+        def end_step(g, state):
+            state = list(state)
+            for u in range(8):
+                dt = dtb3[token(g, u), :]
+                dx = dt * xb3[token(g, u), :]
+                for i in range(8):
+                    n = half * 8 + i
+                    b = bcx[g, pl.ds(u, 1), pl.ds(n * LANES, LANES)]
+                    state[i] = jnp.exp2(dt * a2b[pl.ds(n * 8, 8), :]) * state[i] + dx * b
+            return tuple(state)
+
+        state = lax.fori_loop(0, TOK // 8, end_step, tuple(jnp.zeros((TILES, LANES), F32) for _ in range(8)))
+        for i in range(8):
+            lb[pl.ds(half * 64 + i * 8, 8), :] = state[i]
+        for j in range(0, TILES, 2):
+            two = [lb[pl.ds(half * 64 + j + i, 8, stride=TILES), :] for i in range(2)]
+            l_out[pl.ds(half * 64 + j * 8, 16), :] = jnp.concatenate(two, axis=0).astype(BF16)
+        for d in far_z:
+            to = (mz + d) % 4
+            remote(l_out.at[half_block(half, to), :], l_in.at[half, quarter_of(mz), :], LZ + half, along_z(d)).start()
+        l_in[half, quarter_of(mz), :] = l_out[half_block(half, mq), :]
 
     for i in range(4, 8):
         spread(i)
@@ -365,7 +375,8 @@
     for jj in range(2):
         run = jnp.zeros((1, LANES), F32)
         for z in range(NZ):
-            decay[pl.ds(z * 32 + jj * ST, ST), :] = jnp.exp2(a2s[jj] * s_in[z, jj])
+            for half in range(2):
+                decay[half, pl.ds(z * 16 + jj * 8, 8), :] = jnp.exp2(a2s[half][jj] * s_in[z, jj])
             cum_out[z, jj] = run
             run = run + s_in[z, jj]
         sx_out[jj] = run
@@ -392,22 +403,23 @@
         remote(cum_out.at[(mz + dz + NZ) % NZ], cum_in.at[pair_of(mq)], CZ, along_z(dz)).start()
     cum_in[pair_of(mq)] = cum_out[mz]
 
-    drain(l_in.at[pl.ds(0, 480), :], recv_sem.at[LZ])
-    for jj in range(2):
-        carry = jnp.zeros((ST, LANES), F32)
+    for half in range(2):
+        drain(l_in.at[half, pl.ds(0, 240), :], recv_sem.at[LZ + half])
+        carry = jnp.zeros((16, LANES), F32)
         for z in range(NZ):
-            rows = pl.ds(z * 32 + jj * ST, ST)
-            before[rows, :] = carry.astype(BF16)
-            carry = decay[rows, :] * carry + l_in[rows, :].astype(F32)
-        t_out[pl.ds(jj * ST, ST), :] = carry.astype(BF16)
-
-    @pl.when(mx < NX - 1)
-    def _():
-        to_planes(t_out, t_in.at[mx, block_of(mq)], TX)
-
-    for dz in (-2, -1, 1):
-        remote(before.at[block_of((mz + dz + NZ) % NZ), :], h_in.at[block_of(mq), :], HZ, along_z(dz)).start()
-    h_in[block_of(mq), :] = before[block_of(mz), :]
+            rows = pl.ds(z * 16, 16)
+            before[half, rows, :] = carry.astype(BF16)
+            carry = decay[half, rows, :] * carry + l_in[half, rows, :].astype(F32)
+        t_out[half] = carry.astype(BF16)
+
+        @pl.when(mx < NX - 1)
+        def _():
+            to_planes(t_out.at[half], t_in.at[half, mx, quarter_of(mq)], TX + 3 * half)
+
+        for dz in (-2, -1, 1):
+            to = (mz + dz + NZ) % NZ
+            remote(before.at[half, quarter_of(to), :], h_in.at[half, quarter_of(mq), :], HZ + half, along_z(dz)).start()
+        h_in[half, quarter_of(mq), :] = before[half, quarter_of(mz), :]
 
     carry_x[...] = jnp.zeros_like(carry_x)
     for i in range(NX - 1):
@@ -416,24 +428,28 @@
         def _():
             drain(sx_in.at[i], recv_sem.at[CX + i])
             for j in range(TILES):
-                rows = pl.ds(j * ST, ST)
-                plane[pl.ds(i * 128 + j * ST, ST), :] = jnp.exp2(a2n[rows, :] * sx_in[i, j])
+                for half in range(2):
+                    rows = pl.ds(half * 64 + j * 8, 8)
+                    plane[i, rows, :] = jnp.exp2(a2n[rows, :] * sx_in[i, j])
 
     drain(cum_in.at[pl.ds(0, 6)], recv_sem.at[CZ])
     for j in range(TILES):
-        rows = pl.ds(j * ST, ST)
-        reach[rows, :] = jnp.exp2(a2n[rows, :] * cum_in[j])
-    for i in range(NX - 1):
-
-        @pl.when(i < mx)
-        def _():
-            drain(t_in.at[i], recv_sem.at[TX + i])
-            carry_x[...] = plane[pl.ds(i * 128, 128), :] * carry_x[...] + t_in[i].astype(F32)
-
-    drain(h_in.at[pl.ds(0, 96), :], recv_sem.at[HZ])
-    hf[...] = h_in[...].astype(F32) + reach[...] * carry_x[...]
-
-    carried = [hf[pl.ds(n, TILES, stride=ST), :] for n in range(ST)]
+        for half in range(2):
+            rows = pl.ds(half * 64 + j * 8, 8)
+            reach[rows, :] = jnp.exp2(a2n[rows, :] * cum_in[j])
+    for half in range(2):
+        rows = pl.ds(half * 64, 64)
+        for i in range(NX - 1):
+
+            @pl.when(i < mx)
+            def _():
+                drain(t_in.at[half, i], recv_sem.at[TX + 3 * half + i])
+                carry_x[rows, :] = plane[i, rows, :] * carry_x[rows, :] + t_in[half, i].astype(F32)
+
+        drain(h_in.at[half, pl.ds(0, 48), :], recv_sem.at[HZ + half])
+        hf[rows, :] = h_in[half].astype(F32) + reach[rows, :] * carry_x[rows, :]
+
+    carried = [hf[pl.ds((n // 8) * 64 + n % 8, TILES, stride=8), :] for n in range(ST)]
 
     def add_step(g, _):
         for u in range(8):
@@ -467,16 +483,18 @@
     drain(kz_in.at[pl.ds(0, 240), :], send_sem.at[KZ])
     drain(kx_in.at[pl.ds(0, 96), :], send_sem.at[KX])
     drain(s_in.at[pl.ds(0, NZ - 1)], send_sem.at[SZ])
-    drain(l_in.at[pl.ds(0, 480), :], send_sem.at[LZ])
+    for half in range(2):
+        drain(l_in.at[half, pl.ds(0, 240), :], send_sem.at[LZ + half])
+        drain(h_in.at[half, pl.ds(0, 48), :], send_sem.at[HZ + half])
     for dx in (1, 2, 3):
 
         @pl.when(mx + dx < NX)
         def _():
             drain(sx_in.at[0], send_sem.at[CX + dx - 1])
-            drain(t_in.at[0], send_sem.at[TX + dx - 1])
+            for half in range(2):
+                drain(t_in.at[half, 0], send_sem.at[TX + 3 * half + dx - 1])
 
     drain(cum_in.at[pl.ds(0, 6)], send_sem.at[CZ])
-    drain(h_in.at[pl.ds(0, 96), :], send_sem.at[HZ])
 
 
 def local(
@@ -499,14 +517,14 @@
             V((TOK * TILES, LANES), F32), V((TOK * TILES, LANES), F32), V((TOK // 8, 8, 2 * ST * LANES), F32),
             V((ST * TILES, LANES), F32), V((ST * TILES, LANES), F32), V((ST * TILES, LANES), F32),
             V((TOK * ST * TILES, LANES), F32), V((TOK * TILES, LANES), F32), V((TOK * TILES, LANES), F32), V((TILES, LANES), F32),
-            V((TILES, 1, LANES), F32), V((NZ, 2, 1, LANES), F32), V((ST * TILES, LANES), BF16), V((NZ * 32, LANES), BF16),
+            V((TILES, 1, LANES), F32), V((NZ, 2, 1, LANES), F32), V((128, LANES), BF16), V((2, NZ * 16, LANES), BF16),
             V((2, 1, LANES), F32), V((NX - 1, TILES, 1, LANES), F32), V((NZ, 2, 1, LANES), F32), V((TILES, 1, LANES), F32),
-            V((32, LANES), BF16), V((NX - 1, 128, LANES), BF16), V((NZ * 32, LANES), BF16), V((128, LANES), BF16),
-            V((128, LANES), F32), V((NZ * 32, LANES), F32), V((128, LANES), F32), V(((NX - 1) * 128, LANES), F32),
+            V((2, 16, LANES), BF16), V((2, NX - 1, 64, LANES), BF16), V((2, NZ * 16, LANES), BF16), V((2, 64, LANES), BF16),
+            V((128, LANES), F32), V((2, NZ * 16, LANES), F32), V((128, LANES), F32), V((NX - 1, 128, LANES), F32),
             V((128, LANES), F32),
             V((256, LANES), BF16), V((256, LANES), BF16), V((TOK, 2 * LANES), BF16),
             pltpu.SemaphoreType.DMA((15,)),
-            pltpu.SemaphoreType.DMA((16,)), pltpu.SemaphoreType.DMA((16,)),
+            pltpu.SemaphoreType.DMA((21,)), pltpu.SemaphoreType.DMA((21,)),
             pltpu.SemaphoreType.REGULAR((4,)),
         ],
         compiler_params=pltpu.CompilerParams(

time: 40.4 us -> 41 us (1.015)
  Pallas kernels: 38.3 us -> 38.9 us
    pallas_call x1, Pallas kernels: 38.3 us -> 38.9 us  [local(): pl.pallas_call(kernel, out_shape=(pltpu.VMEM((TOK, CH), BF16), pltpu.VMEM...]
where the time goes in v5:
time: 41 us; the launch traced here: 40.9 us
  Pallas kernels  38.9 us (95%)
  local copies, waits for them, and re-layouts  1.33 us (3%)
  between operations  0.64 us (2%)
    pallas_call x1, Pallas kernels, local(): pl.pallas_call(kernel, out_shape=(pltpu.VMEM((TOK, CH), BF16), pltpu.VMEM...  38.9 us
    unnamed x2, local copies, waits for them, and re-layouts  1.33 us

profile of v5, /device:TPU:2, one launch (start us, length us, event | category | flops | bytes accessed | tf_op | source)
XLA Modules:
  0.0 40.9 jit_solution(16712831412022602055)
XLA Ops:
  0.6 38.9 %shard_map.140 = (bf16[128,1024]{1,0:T(8,128)(2,1)S(1)}, bf16[1,128,256]{2,1,0:T(8,128)(2,1)S(1)}) custom-call(bf16[128,1024]{1,0:T(8,128)(2,1)} %x_hbm.1, bf16[128,1024]{1,0:T(8,128)(2,1)} %gate_hbm.1, f32[4,1024]{1,0:T(4,128)} %cw_hbm.1, f32[1,1024]{1,0:T(1,128)} %bitcast.6, bf16[1024,256]{1,0:T(8,128)(2,1)} %low_hbm.1, bf16[32,1024]{1,0:T(8,128)(2,1)} %bitcast.5, ...), custom_call_target="tpu_custom_call" | custom-call | tf_op jit(solution)/shard_map/pallas_call | solution.py:506
  39.5 0.7 %copy.17 = bf16[128,1024]{1,0:T(8,128)(2,1)} copy(bf16[128,1024]{1,0:T(8,128)(2,1)S(1)} %get-tuple-element.2) | data formatting | bytes 524288
  40.2 0.6 %copy.18 = bf16[1,128,256]{2,1,0:T(8,128)(2,1)} copy(bf16[1,128,256]{2,1,0:T(8,128)(2,1)S(1)} %get-tuple-element.3) | data formatting | bytes 131072

commit v6 on v5

--- a/solution.py
+++ b/solution.py
@@ -9,6 +9,7 @@
 from jax.sharding import PartitionSpec as P
 
 MOST = 2
+PARTS = 4
 NZ = 16
 NX = 4
 NC = 8
@@ -43,15 +44,15 @@
 
 def kernel(
     x_hbm, gate_hbm, cw_hbm, cb_hbm, low_hbm, bc_hbm, dtw_hbm, dtb_hbm, dec_hbm, skip_hbm, kv_hbm, idx_hbm, own_hbm,
-    gated_out, kept_out,
+    gb, yb, hf, kept_out,
     x_v, gate_v, cw_v, cb_v, low_v, bc_v, dtw_v, dtb_v, dec_v, skip_v, kv_v, idx_v, own_v, decs_v,
-    halo, halo_out, halo_f, xs, act, part, rs_in, r0_in, ag_out, lr, dtb3, xb3, bcx, a2b, a2n, lb, gb, yb, sgb, skip_b,
-    s_out, s_in, l_out, l_in, sx_out, sx_in, cum_out, cum_in, t_out, t_in, before, h_in, hf, decay, reach,
+    halo, halo_out, halo_f, xs, act, part, rs_in, r0_in, ag_out, lr, dtb3, xb3, bcx, a2b, a2n, lb, sgb, skip_b,
+    s_out, s_in, l_out, l_in, sx_out, sx_in, cum_out, cum_in, t_out, t_in, before, h_in, decay, reach,
     plane, carry_x,
     kz_out, kz_in, kx_out,
     in_sem, send_sem, recv_sem, here_sem,
 ):
-    kx_in = kept_out.at[0]
+    kx_in = kept_out
     me = lax.axis_index("ctx")
     mc = lax.axis_index("ch")
     mx = me // NZ
@@ -449,23 +450,6 @@
         drain(h_in.at[half, pl.ds(0, 48), :], recv_sem.at[HZ + half])
         hf[rows, :] = h_in[half].astype(F32) + reach[rows, :] * carry_x[rows, :]
 
-    carried = [hf[pl.ds((n // 8) * 64 + n % 8, TILES, stride=8), :] for n in range(ST)]
-
-    def add_step(g, _):
-        for u in range(8):
-            at = token(g, u)
-            y = [yb[at, :], None, None, None]
-            for n in range(ST):
-                term = gb[pl.ds(pl.multiple_of(g * 1024, 1024) + u * 128 + n * 8, 8), :] * carried[n]
-                y[n % 4] = term if y[n % 4] is None else y[n % 4] + term
-            yb[at, :] = (y[0] + y[1]) + (y[2] + y[3])
-        return 0
-
-    lax.fori_loop(0, TOK // 8, add_step, 0)
-
-    for j in range(TILES):
-        cols = pl.ds(j * LANES, LANES)
-        gated_out[:, cols] = yb[pl.ds(j, TOK, stride=TILES), :].astype(BF16)
     drain(kx_in.at[pl.ds(0, 96), :], recv_sem.at[KX])
 
     drain(halo, send_sem.at[HALO])
@@ -497,17 +481,51 @@
     drain(cum_in.at[pl.ds(0, 6)], send_sem.at[CZ])
 
 
+def finish(gb, yb, hf, kept, gated_hbm, kept_hbm, ys, gated_v, sem):
+    kept_copy = pltpu.make_async_copy(kept, kept_hbm.at[0], sem.at[PARTS])
+    kept_copy.start()
+    carried = [hf[pl.ds((n // 8) * 64 + n % 8, TILES, stride=8), :] for n in range(ST)]
+    rows = TOK // PARTS
+    copies = []
+    for part in range(PARTS):
+
+        def add_step(g, _):
+            for u in range(8):
+                at = pl.ds(pl.multiple_of(g * 64, 64) + u * 8, 8)
+                y = [yb[at, :], None, None, None]
+                for n in range(ST):
+                    term = gb[pl.ds(pl.multiple_of(g * 1024, 1024) + u * 128 + n * 8, 8), :] * carried[n]
+                    y[n % 4] = term if y[n % 4] is None else y[n % 4] + term
+                ys[at, :] = (y[0] + y[1]) + (y[2] + y[3])
+            return 0
+
+        lax.fori_loop(part * rows // 8, (part + 1) * rows // 8, add_step, 0)
+        here = pl.ds(part * rows, rows)
+        for j in range(TILES):
+            y = ys[pl.ds(part * rows * TILES + j, rows, stride=TILES), :]
+            gated_v[here, pl.ds(j * LANES, LANES)] = y.astype(BF16)
+        copies.append(pltpu.make_async_copy(gated_v.at[here, :], gated_hbm.at[here, :], sem.at[part]))
+        copies[-1].start()
+    for c in copies:
+        c.wait()
+    kept_copy.wait()
+
+
 def local(
     x_in, gate_in, conv_weight, conv_bias, proj_low, proj_bc, dt_weight, dt_bias, decay_log, skip_gain, attn_kv,
     kept_index, kept_owner,
 ):
     V = pltpu.VMEM
     hbm = pl.BlockSpec(memory_space=pltpu.HBM)
-    return pl.pallas_call(
+    vmem = pl.BlockSpec(memory_space=pltpu.VMEM)
+    pin = functools.partial(pltpu.with_memory_space_constraint, memory_space=pltpu.HBM)
+    parts = pl.pallas_call(
         kernel,
-        out_shape=(pltpu.VMEM((TOK, CH), BF16), pltpu.VMEM((1, TOK, 2 * LANES), BF16)),
+        out_shape=(
+            V((TOK * ST * TILES, LANES), F32), V((TOK * TILES, LANES), F32), V((128, LANES), F32), V((TOK, 2 * LANES), BF16),
+        ),
         in_specs=[hbm] * 13,
-        out_specs=(pl.BlockSpec(memory_space=pltpu.VMEM),) * 2,
+        out_specs=(vmem,) * 4,
         scratch_shapes=[
             V((TOK, CH), BF16), V((TOK, CH), BF16), V((CONV, CH), F32), V((1, CH), F32), V((CH, RANK), BF16),
             V((LANES, CH), BF16), V((RANK, CH), BF16), V((1, CH), F32), V((ST, CH), F32), V((1, CH), F32),
@@ -516,11 +534,11 @@
             V((TOK, RANK + LANES), BF16), V((TOK, RANK + LANES), BF16), V((TOK, RANK + LANES), BF16), V((16, RANK + LANES), BF16), V((TOK, RANK + LANES), BF16),
             V((TOK * TILES, LANES), F32), V((TOK * TILES, LANES), F32), V((TOK // 8, 8, 2 * ST * LANES), F32),
             V((ST * TILES, LANES), F32), V((ST * TILES, LANES), F32), V((ST * TILES, LANES), F32),
-            V((TOK * ST * TILES, LANES), F32), V((TOK * TILES, LANES), F32), V((TOK * TILES, LANES), F32), V((TILES, LANES), F32),
+            V((TOK * TILES, LANES), F32), V((TILES, LANES), F32),
             V((TILES, 1, LANES), F32), V((NZ, 2, 1, LANES), F32), V((128, LANES), BF16), V((2, NZ * 16, LANES), BF16),
             V((2, 1, LANES), F32), V((NX - 1, TILES, 1, LANES), F32), V((NZ, 2, 1, LANES), F32), V((TILES, 1, LANES), F32),
             V((2, 16, LANES), BF16), V((2, NX - 1, 64, LANES), BF16), V((2, NZ * 16, LANES), BF16), V((2, 64, LANES), BF16),
-            V((128, LANES), F32), V((2, NZ * 16, LANES), F32), V((128, LANES), F32), V((NX - 1, 128, LANES), F32),
+            V((2, NZ * 16, LANES), F32), V((128, LANES), F32), V((NX - 1, 128, LANES), F32),
             V((128, LANES), F32),
             V((256, LANES), BF16), V((256, LANES), BF16), V((TOK, 2 * LANES), BF16),
             pltpu.SemaphoreType.DMA((15,)),
@@ -528,12 +546,22 @@
             pltpu.SemaphoreType.REGULAR((4,)),
         ],
         compiler_params=pltpu.CompilerParams(
-            collective_id=0, has_side_effects=True, vmem_limit_bytes=62_000_000
+            collective_id=0, has_side_effects=True, vmem_limit_bytes=40_000_000
         ),
-    )(
+    )(*map(pin, (
         x_in, gate_in, conv_weight, conv_bias.reshape(1, CH), proj_low, proj_bc.T, dt_weight, dt_bias.reshape(1, CH),
         decay_log, skip_gain.reshape(1, CH), attn_kv, kept_index, kept_owner.reshape(1, KEEP),
-    )
+    )))
+    return pl.pallas_call(
+        finish,
+        out_shape=(jax.ShapeDtypeStruct((TOK, CH), BF16), jax.ShapeDtypeStruct((1, TOK, 2 * LANES), BF16)),
+        in_specs=[vmem] * 4,
+        out_specs=(hbm, hbm),
+        scratch_shapes=[
+            V((TOK * TILES, LANES), F32), V((TOK, CH), BF16), pltpu.SemaphoreType.DMA((PARTS + 1,)),
+        ],
+        compiler_params=pltpu.CompilerParams(vmem_limit_bytes=20_000_000),
+    )(*parts)
 
 
 def solution(mesh):

time: 41 us -> 40.4 us (0.985)
  local copies, waits for them, and re-layouts: 1.33 us -> 0 us
  Pallas kernels: 38.9 us -> 39.6 us
    unnamed x2 -> x0, local copies, waits for them, and re-layouts: 1.33 us -> none
    pallas_call x1 -> x2, Pallas kernels: 38.9 us -> 39.6 us  [the longest x1 38.2 us: local(): pl.pallas_call(kernel, out_shape=(V((TOK * ST * TILES, LANES), F32), V((T...]
where the time goes in v6:
time: 40.4 us; the launch traced here: 40.3 us
  Pallas kernels  39.6 us (98%)
  between operations  0.64 us (2%)
    pallas_call x1, Pallas kernels, local(): pl.pallas_call(kernel, out_shape=(V((TOK * ST * TILES, LANES), F32), V((T...  38.2 us
    pallas_call x1, Pallas kernels, local(): pl.pallas_call(finish, out_shape=(jax.ShapeDtypeStruct((TOK, CH), BF16),...  1.44 us

profile of v6, /device:TPU:2, one launch (start us, length us, event | category | flops | bytes accessed | tf_op | source)
XLA Modules:
  0.0 40.3 jit_solution(7918761465482453650)
XLA Ops:
  0.6 38.2 %shard_map.140 = (f32[16384,128]{1,0:T(8,128)S(1)}, f32[1024,128]{1,0:T(8,128)S(1)}, f32[128,128]{1,0:T(8,128)S(1)}, bf16[128,256]{1,0:T(8,128)(2,1)S(1)}) custom-call(bf16[128,1024]{1,0:T(8,128)(2,1)} %x_hbm.1, bf16[128,1024]{1,0:T(8,128)(2,1)} %gate_hbm.1, f32[4,1024]{1,0:T(4,128)} %cw_hbm.1, f32[1,1024]{1,0:T(1,128)} %bitcast.6, ...), custom_call_target="tpu_custom_call" | custom-call | tf_op jit(solution)/shard_map/pallas_call | solution.py:522
  38.8 1.4 %shard_map.141 = (bf16[128,1024]{1,0:T(8,128)(2,1)}, bf16[1,128,256]{2,1,0:T(8,128)(2,1)}) custom-call(f32[16384,128]{1,0:T(8,128)S(1)} %get-tuple-element.6.gb, f32[1024,128]{1,0:T(8,128)S(1)} %get-tuple-element.7.yb, f32[128,128]{1,0:T(8,128)S(1)} %get-tuple-element.8.hf, bf16[128,256]{1,0:T(8,128)(2,1)S(1)} %get-tuple-element.9.kept), custom_call_target="tpu_custom_call" | custom-call | tf_op jit(solution)/shard_map/pallas_call | solution.py:555

commit v7 on v4

--- a/solution.py
+++ b/solution.py
@@ -9,6 +9,7 @@
 from jax.sharding import PartitionSpec as P
 
 MOST = 2
+PARTS = 4
 NZ = 16
 NX = 4
 NC = 8
@@ -43,15 +44,15 @@
 
 def kernel(
     x_hbm, gate_hbm, cw_hbm, cb_hbm, low_hbm, bc_hbm, dtw_hbm, dtb_hbm, dec_hbm, skip_hbm, kv_hbm, idx_hbm, own_hbm,
-    gated_out, kept_out,
+    gb, yb, hf, kept_out,
     x_v, gate_v, cw_v, cb_v, low_v, bc_v, dtw_v, dtb_v, dec_v, skip_v, kv_v, idx_v, own_v, decs_v,
-    halo, halo_out, halo_f, xs, act, part, rs_in, r0_in, ag_out, lr, dtb3, xb3, bcx, a2b, a2n, lb, gb, yb, sgb, skip_b,
-    s_out, s_in, l_out, l_in, sx_out, sx_in, cum_out, cum_in, t_out, t_in, before, h_in, hf, decay, reach,
+    halo, halo_out, halo_f, xs, act, part, rs_in, r0_in, ag_out, lr, dtb3, xb3, bcx, a2b, a2n, lb, sgb, skip_b,
+    s_out, s_in, l_out, l_in, sx_out, sx_in, cum_out, cum_in, t_out, t_in, before, h_in, decay, reach,
     plane, carry_x,
     kz_out, kz_in, kx_out,
     in_sem, send_sem, recv_sem, here_sem,
 ):
-    kx_in = kept_out.at[0]
+    kx_in = kept_out
     me = lax.axis_index("ctx")
     mc = lax.axis_index("ch")
     mx = me // NZ
@@ -68,7 +69,7 @@
     loads = [pltpu.make_async_copy(s, d, in_sem.at[i]) for i, (s, d) in enumerate(loads)]
     (x_ld, cw_ld, cb_ld, idx_ld, own_ld, kv_ld, low_ld, bc_ld, bc2_ld, dec_ld, decs_ld, dtw_ld, dtb_ld, skip_ld, gate_ld) = loads
 
-    for c in loads:
+    for c in loads[:3]:
         c.start()
 
     def along_z(d):
@@ -103,6 +104,9 @@
     @pl.when(mz == 0)
     def _():
         pl.semaphore_signal(barrier, inc=1, device_id=left)
+
+    for c in loads[3:]:
+        c.start()
 
     def tell(i):
         for d in (-(1 << i), 1 << i):
@@ -265,7 +269,9 @@
     for j in range(TILES):
         cols = pl.ds(j * LANES, LANES)
         v = dot(lr[:, pl.ds(0, RANK)], dtw_v[:, cols]) + dtb_v[:, cols]
-        dtb3[pl.ds(j, TOK, stride=TILES), :] = jnp.maximum(v, 0.0) + jnp.log1p(jnp.exp(-jnp.abs(v)))
+        v = jnp.maximum(v, 0.0) + jnp.log1p(jnp.exp(-jnp.abs(v)))
+        dtb3[pl.ds(j, TOK, stride=TILES), :] = v
+        s_out[j] = jnp.sum(v, axis=0, keepdims=True)
     coeff = lr[:, pl.ds(RANK, LANES)]
 
     def spread(i):
@@ -279,14 +285,6 @@
     def token(g, u):
         return pl.ds(pl.multiple_of(g * 64, 64) + u * 8, 8)
 
-    def total_step(g, acc):
-        for u in range(8):
-            acc = acc + dtb3[token(g, u), :]
-        return acc
-
-    s_total = lax.fori_loop(0, TOK // 8, total_step, jnp.zeros((TILES, LANES), F32))
-    for j in range(TILES):
-        s_out[j] = s_total[j : j + 1, :]
     for d in far_z:
         to = (mz + d) % 4
         remote(s_out.at[pl.ds(2 * to, 2)], s_in.at[mz], SZ, along_z(d)).start()
@@ -433,23 +431,6 @@
     drain(h_in.at[pl.ds(0, 96), :], recv_sem.at[HZ])
     hf[...] = h_in[...].astype(F32) + reach[...] * carry_x[...]
 
-    carried = [hf[pl.ds(n, TILES, stride=ST), :] for n in range(ST)]
-
-    def add_step(g, _):
-        for u in range(8):
-            at = token(g, u)
-            y = [yb[at, :], None, None, None]
-            for n in range(ST):
-                term = gb[pl.ds(pl.multiple_of(g * 1024, 1024) + u * 128 + n * 8, 8), :] * carried[n]
-                y[n % 4] = term if y[n % 4] is None else y[n % 4] + term
-            yb[at, :] = (y[0] + y[1]) + (y[2] + y[3])
-        return 0
-
-    lax.fori_loop(0, TOK // 8, add_step, 0)
-
-    for j in range(TILES):
-        cols = pl.ds(j * LANES, LANES)
-        gated_out[:, cols] = yb[pl.ds(j, TOK, stride=TILES), :].astype(BF16)
     drain(kx_in.at[pl.ds(0, 96), :], recv_sem.at[KX])
 
     drain(halo, send_sem.at[HALO])
@@ -477,6 +458,36 @@
 
     drain(cum_in.at[pl.ds(0, 6)], send_sem.at[CZ])
     drain(h_in.at[pl.ds(0, 96), :], send_sem.at[HZ])
+
+
+def finish(gb, yb, hf, kept, gated_hbm, kept_hbm, ys, gated_v, sem):
+    kept_copy = pltpu.make_async_copy(kept, kept_hbm.at[0], sem.at[PARTS])
+    kept_copy.start()
+    carried = [hf[pl.ds(n, TILES, stride=ST), :] for n in range(ST)]
+    rows = TOK // PARTS
+    copies = []
+    for part in range(PARTS):
+
+        def add_step(g, _):
+            for u in range(8):
+                at = pl.ds(pl.multiple_of(g * 64, 64) + u * 8, 8)
+                y = [yb[at, :], None, None, None]
+                for n in range(ST):
+                    term = gb[pl.ds(pl.multiple_of(g * 1024, 1024) + u * 128 + n * 8, 8), :] * carried[n]
+                    y[n % 4] = term if y[n % 4] is None else y[n % 4] + term
+                ys[at, :] = (y[0] + y[1]) + (y[2] + y[3])
+            return 0
+
+        lax.fori_loop(part * rows // 8, (part + 1) * rows // 8, add_step, 0)
+        here = pl.ds(part * rows, rows)
+        for j in range(TILES):
+            y = ys[pl.ds(part * rows * TILES + j, rows, stride=TILES), :]
+            gated_v[here, pl.ds(j * LANES, LANES)] = y.astype(BF16)
+        copies.append(pltpu.make_async_copy(gated_v.at[here, :], gated_hbm.at[here, :], sem.at[part]))
+        copies[-1].start()
+    for c in copies:
+        c.wait()
+    kept_copy.wait()
 
 
 def local(
@@ -485,11 +496,15 @@
 ):
     V = pltpu.VMEM
     hbm = pl.BlockSpec(memory_space=pltpu.HBM)
-    return pl.pallas_call(
+    vmem = pl.BlockSpec(memory_space=pltpu.VMEM)
+    pin = functools.partial(pltpu.with_memory_space_constraint, memory_space=pltpu.HBM)
+    parts = pl.pallas_call(
         kernel,
-        out_shape=(pltpu.VMEM((TOK, CH), BF16), pltpu.VMEM((1, TOK, 2 * LANES), BF16)),
+        out_shape=(
+            V((TOK * ST * TILES, LANES), F32), V((TOK * TILES, LANES), F32), V((128, LANES), F32), V((TOK, 2 * LANES), BF16),
+        ),
         in_specs=[hbm] * 13,
-        out_specs=(pl.BlockSpec(memory_space=pltpu.VMEM),) * 2,
+        out_specs=(vmem,) * 4,
         scratch_shapes=[
             V((TOK, CH), BF16), V((TOK, CH), BF16), V((CONV, CH), F32), V((1, CH), F32), V((CH, RANK), BF16),
             V((LANES, CH), BF16), V((RANK, CH), BF16), V((1, CH), F32), V((ST, CH), F32), V((1, CH), F32),
@@ -498,11 +513,11 @@
             V((TOK, RANK + LANES), BF16), V((TOK, RANK + LANES), BF16), V((TOK, RANK + LANES), BF16), V((16, RANK + LANES), BF16), V((TOK, RANK + LANES), BF16),
             V((TOK * TILES, LANES), F32), V((TOK * TILES, LANES), F32), V((TOK // 8, 8, 2 * ST * LANES), F32),
             V((ST * TILES, LANES), F32), V((ST * TILES, LANES), F32), V((ST * TILES, LANES), F32),
-            V((TOK * ST * TILES, LANES), F32), V((TOK * TILES, LANES), F32), V((TOK * TILES, LANES), F32), V((TILES, LANES), F32),
+            V((TOK * TILES, LANES), F32), V((TILES, LANES), F32),
             V((TILES, 1, LANES), F32), V((NZ, 2, 1, LANES), F32), V((ST * TILES, LANES), BF16), V((NZ * 32, LANES), BF16),
             V((2, 1, LANES), F32), V((NX - 1, TILES, 1, LANES), F32), V((NZ, 2, 1, LANES), F32), V((TILES, 1, LANES), F32),
             V((32, LANES), BF16), V((NX - 1, 128, LANES), BF16), V((NZ * 32, LANES), BF16), V((128, LANES), BF16),
-            V((128, LANES), F32), V((NZ * 32, LANES), F32), V((128, LANES), F32), V(((NX - 1) * 128, LANES), F32),
+            V((NZ * 32, LANES), F32), V((128, LANES), F32), V(((NX - 1) * 128, LANES), F32),
             V((128, LANES), F32),
             V((256, LANES), BF16), V((256, LANES), BF16), V((TOK, 2 * LANES), BF16),
             pltpu.SemaphoreType.DMA((15,)),
@@ -510,12 +525,22 @@
             pltpu.SemaphoreType.REGULAR((4,)),
         ],
         compiler_params=pltpu.CompilerParams(
-            collective_id=0, has_side_effects=True, vmem_limit_bytes=62_000_000
+            collective_id=0, has_side_effects=True, vmem_limit_bytes=40_000_000
         ),
-    )(
+    )(*map(pin, (
         x_in, gate_in, conv_weight, conv_bias.reshape(1, CH), proj_low, proj_bc.T, dt_weight, dt_bias.reshape(1, CH),
         decay_log, skip_gain.reshape(1, CH), attn_kv, kept_index, kept_owner.reshape(1, KEEP),
-    )
+    )))
+    return pl.pallas_call(
+        finish,
+        out_shape=(jax.ShapeDtypeStruct((TOK, CH), BF16), jax.ShapeDtypeStruct((1, TOK, 2 * LANES), BF16)),
+        in_specs=[vmem] * 4,
+        out_specs=(hbm, hbm),
+        scratch_shapes=[
+            V((TOK * TILES, LANES), F32), V((TOK, CH), BF16), pltpu.SemaphoreType.DMA((PARTS + 1,)),
+        ],
+        compiler_params=pltpu.CompilerParams(vmem_limit_bytes=20_000_000),
+    )(*parts)
 
 
 def solution(mesh):

time: 40.4 us -> 39.5 us (0.978)
  local copies, waits for them, and re-layouts: 1.33 us -> 0 us
    unnamed x2 -> x0, local copies, waits for them, and re-layouts: 1.33 us -> none
    pallas_call x1 -> x2, Pallas kernels: 38.3 us -> 38.7 us  [the longest x1 37.3 us: local(): pl.pallas_call(kernel, out_shape=(V((TOK * ST * TILES, LANES), F32), V((T...]
where the time goes in v7:
time: 39.5 us; the launch traced here: 39.4 us
  Pallas kernels  38.7 us (98%)
  between operations  0.64 us (2%)
    pallas_call x1, Pallas kernels, local(): pl.pallas_call(kernel, out_shape=(V((TOK * ST * TILES, LANES), F32), V((T...  37.3 us
    pallas_call x1, Pallas kernels, local(): pl.pallas_call(finish, out_shape=(jax.ShapeDtypeStruct((TOK, CH), BF16),...  1.45 us

profile of v7, /device:TPU:2, one launch (start us, length us, event | category | flops | bytes accessed | tf_op | source)
XLA Modules:
  0.0 39.4 jit_solution(6307051992934273672)
XLA Ops:
  0.6 37.3 %shard_map.140 = (f32[16384,128]{1,0:T(8,128)S(1)}, f32[1024,128]{1,0:T(8,128)S(1)}, f32[128,128]{1,0:T(8,128)S(1)}, bf16[128,256]{1,0:T(8,128)(2,1)S(1)}) custom-call(bf16[128,1024]{1,0:T(8,128)(2,1)} %x_hbm.1, bf16[128,1024]{1,0:T(8,128)(2,1)} %gate_hbm.1, f32[4,1024]{1,0:T(4,128)} %cw_hbm.1, f32[1,1024]{1,0:T(1,128)} %bitcast.6, ...), custom_call_target="tpu_custom_call" | custom-call | tf_op jit(solution)/shard_map/pallas_call | solution.py:501
  37.9 1.4 %shard_map.141 = (bf16[128,1024]{1,0:T(8,128)(2,1)}, bf16[1,128,256]{2,1,0:T(8,128)(2,1)}) custom-call(f32[16384,128]{1,0:T(8,128)S(1)} %get-tuple-element.6.gb, f32[1024,128]{1,0:T(8,128)S(1)} %get-tuple-element.7.yb, f32[128,128]{1,0:T(8,128)S(1)} %get-tuple-element.8.hf, bf16[128,256]{1,0:T(8,128)(2,1)S(1)} %get-tuple-element.9.kept), custom_call_target="tpu_custom_call" | custom-call | tf_op jit(solution)/shard_map/pallas_call | solution.py:534

commit v8 on v7

--- a/solution.py
+++ b/solution.py
@@ -200,6 +200,20 @@
         remote(part.at[pl.ds(0, 16), :], r0_in.at[rows_of(mc), :], R0, along_ch(*d)).start()
     r0_in[rows_of(mc), :] = part[pl.ds(0, 16), :]
 
+    hear(1)
+    tell(2)
+
+    @pl.when(mc > 0)
+    def _():
+        rs_in[rows_of(mc), :] = part[rows_of(mc), :]
+        drain(rs_in.at[pl.ds(0, TOK - 16), :], recv_sem.at[RS])
+        low, coeff = summed(rs_in)
+        ag_out[:, pl.ds(0, RANK)] = low
+        ag_out[:, pl.ds(RANK, LANES)] = coeff
+        for d in far_ch:
+            remote(ag_out, lr.at[rows_of(mc), :], AG, along_ch(*d)).start()
+        lr[rows_of(mc), :] = ag_out[...]
+
     idx_ld.wait()
     own_ld.wait()
     kv_ld.wait()
@@ -216,9 +230,6 @@
     kz = kz + dot_rows((slots == place + 8).astype(F32).astype(BF16), picked[:, LANES:])
     kz_out[...] = kz.astype(BF16)
 
-    hear(1)
-    tell(2)
-
     dec_ld.wait()
     decs_ld.wait()
     gate_ld.wait()
@@ -232,17 +243,6 @@
         cols = pl.ds(j * LANES, LANES)
         sgb[pl.ds(j, TOK, stride=TILES), :] = silu(gate_v[:, cols].astype(F32))
         skip_b[pl.ds(j, 1), :] = skip_v[:, cols]
-
-    @pl.when(mc > 0)
-    def _():
-        rs_in[rows_of(mc), :] = part[rows_of(mc), :]
-        drain(rs_in.at[pl.ds(0, TOK - 16), :], recv_sem.at[RS])
-        low, coeff = summed(rs_in)
-        ag_out[:, pl.ds(0, RANK)] = low
-        ag_out[:, pl.ds(RANK, LANES)] = coeff
-        for d in far_ch:
-            remote(ag_out, lr.at[rows_of(mc), :], AG, along_ch(*d)).start()
-        lr[rows_of(mc), :] = ag_out[...]
 
     hear(2)
     hear_x()

time: 39.5 us -> 39.8 us (level)
  no operation moved by 1% of the time
where the time goes in v8:
time: 39.8 us; the launch traced here: 39.7 us
  Pallas kernels  39 us (98%)
  between operations  0.64 us (2%)
    pallas_call x1, Pallas kernels, local(): pl.pallas_call(kernel, out_shape=(V((TOK * ST * TILES, LANES), F32), V((T...  37.6 us
    pallas_call x1, Pallas kernels, local(): pl.pallas_call(finish, out_shape=(jax.ShapeDtypeStruct((TOK, CH), BF16),...  1.45 us

profile of v8, /device:TPU:2, one launch (start us, length us, event | category | flops | bytes accessed | tf_op | source)
XLA Modules:
  0.0 39.7 jit_solution(6936247431321109434)
XLA Ops:
  0.6 37.6 %shard_map.140 = (f32[16384,128]{1,0:T(8,128)S(1)}, f32[1024,128]{1,0:T(8,128)S(1)}, f32[128,128]{1,0:T(8,128)S(1)}, bf16[128,256]{1,0:T(8,128)(2,1)S(1)}) custom-call(bf16[128,1024]{1,0:T(8,128)(2,1)} %x_hbm.1, bf16[128,1024]{1,0:T(8,128)(2,1)} %gate_hbm.1, f32[4,1024]{1,0:T(4,128)} %cw_hbm.1, f32[1,1024]{1,0:T(1,128)} %bitcast.6, ...), custom_call_target="tpu_custom_call" | custom-call | tf_op jit(solution)/shard_map/pallas_call | solution.py:501
  38.2 1.4 %shard_map.141 = (bf16[128,1024]{1,0:T(8,128)(2,1)}, bf16[1,128,256]{2,1,0:T(8,128)(2,1)}) custom-call(f32[16384,128]{1,0:T(8,128)S(1)} %get-tuple-element.6.gb, f32[1024,128]{1,0:T(8,128)S(1)} %get-tuple-element.7.yb, f32[128,128]{1,0:T(8,128)S(1)} %get-tuple-element.8.hf, bf16[128,256]{1,0:T(8,128)(2,1)S(1)} %get-tuple-element.9.kept), custom_call_target="tpu_custom_call" | custom-call | tf_op jit(solution)/shard_map/pallas_call | solution.py:534

commit v9 on v7

--- a/solution.py
+++ b/solution.py
@@ -138,11 +138,6 @@
     for j in range(TILES):
         halo_f[pl.ds(4 * j, 4), :] = x_v[pl.ds(TOK - 16, 16), pl.ds(j * LANES, LANES)].astype(F32)[12:, :]
     halo_out[...] = halo_f[...].astype(BF16)
-    pl.semaphore_wait(barrier, NC - 1 + NX - 1 + 2 + jnp.where((mz == 0) | (mz == NZ - 1), 1, 0))
-
-    remote(halo_out, halo, HALO, right).start()
-    tell(0)
-
     def conv(first, rows):
         for j in range(TILES):
             cols = pl.ds(j * LANES, LANES)
@@ -179,6 +174,11 @@
     bc_ld.wait()
     bc2_ld.wait()
     project(16, TOK - 16)
+
+    pl.semaphore_wait(barrier, NC - 1 + NX - 1 + 2 + jnp.where((mz == 0) | (mz == NZ - 1), 1, 0))
+
+    remote(halo_out, halo, HALO, right).start()
+    tell(0)
 
     for d in far_ch:
         to = along_ch(*d)

time: 39.5 us -> 39.6 us (level)
  the two profiles are of different devices: /device:TPU:2 before, /device:TPU:1 now
where the time goes in v9:
time: 39.6 us; the launch traced here: 39.5 us
  Pallas kernels  38.8 us (98%)
  between operations  0.64 us (2%)
    pallas_call x1, Pallas kernels, local(): pl.pallas_call(kernel, out_shape=(V((TOK * ST * TILES, LANES), F32), V((T...  37.4 us
    pallas_call x1, Pallas kernels, local(): pl.pallas_call(finish, out_shape=(jax.ShapeDtypeStruct((TOK, CH), BF16),...  1.45 us

profile of v9, /device:TPU:1, one launch (start us, length us, event | category | flops | bytes accessed | tf_op | source)
XLA Modules:
  0.0 39.5 jit_solution(12039203600920219369)
XLA Ops:
  0.6 37.4 %shard_map.140 = (f32[16384,128]{1,0:T(8,128)S(1)}, f32[1024,128]{1,0:T(8,128)S(1)}, f32[128,128]{1,0:T(8,128)S(1)}, bf16[128,256]{1,0:T(8,128)(2,1)S(1)}) custom-call(bf16[128,1024]{1,0:T(8,128)(2,1)} %x_hbm.1, bf16[128,1024]{1,0:T(8,128)(2,1)} %gate_hbm.1, f32[4,1024]{1,0:T(4,128)} %cw_hbm.1, f32[1,1024]{1,0:T(1,128)} %bitcast.6, ...), custom_call_target="tpu_custom_call" | custom-call | tf_op jit(solution)/shard_map/pallas_call | solution.py:501
  38.0 1.4 %shard_map.141 = (bf16[128,1024]{1,0:T(8,128)(2,1)}, bf16[1,128,256]{2,1,0:T(8,128)(2,1)}) custom-call(f32[16384,128]{1,0:T(8,128)S(1)} %get-tuple-element.6.gb, f32[1024,128]{1,0:T(8,128)S(1)} %get-tuple-element.7.yb, f32[128,128]{1,0:T(8,128)S(1)} %get-tuple-element.8.hf, bf16[128,256]{1,0:T(8,128)(2,1)S(1)} %get-tuple-element.9.kept), custom_call_target="tpu_custom_call" | custom-call | tf_op jit(solution)/shard_map/pallas_call | solution.py:534
